TPU v7x, 768 devices: a whole 4x8x12 slice. The times are simulated.
768 devices in a mesh: band: 8 (over y), lon: 96 (over x, z, core).
Axes of the slice: x: 4, y: 8, z: 12, core: 2. Of those that a mesh axis runs over, the one named last changes fastest.
Arguments:
- grid_latent: bfloat16 [786432, 512], P(('band', 'lon')), may hold values from -6 to 6
- mesh_latent: bfloat16 [98304, 512], P(('band', 'lon')), may hold values from -6 to 6
- mesh_cotangent: bfloat16 [98304, 512], P(('band', 'lon')), may hold values from -6 to 6
- w_grid: bfloat16 [512, 512], replicated, may hold values from -0.25 to 0.25
- w_mesh: bfloat16 [512, 512], replicated, may hold values from -0.25 to 0.25
- w_out: bfloat16 [512, 512], replicated, may hold values from -0.25 to 0.25
- edge_source: int32 [1572864], P(('band', 'lon')), may hold values from 0 to 1023
- edge_target: int32 [1572864], P(('band', 'lon')), may hold values from 0 to 98303, as said below
- edge_count: int32 [768], P(('band', 'lon')), may hold values from 256 to 2048, as said below
Outputs:
- grid_grad: bfloat16 [786432, 512], P(('band', 'lon'))
- mesh_grad: bfloat16 [98304, 512], P(('band', 'lon'))
- weight_grads: float32 [1536, 512], P('lon')
Inputs may be any that keep to these rules, and one draw needn't show every extreme that they name: `edge_target`: the mesh node of a slot of device block d lies in mesh block d or in the next lon block of the same band, with wrap: rows ((band index) * 96 + (lon index + 0 or 1) % 96) * 128 to that plus 128 - 1. `edge_count`: some device has exactly 2048 live slots.
All inputs are finite; a program needn't handle non-finite values.
Results may differ from a plain program's by a relative error of at most 0.015.
Values may be sent and summed in bfloat16 or wider, within the bound.
A program may use at most 32 MiB of HBM per device.

v0:
```python
import jax
import jax.numpy as jnp
from jax import lax
from jax.sharding import PartitionSpec as P


def shifted(block, axis, distance):
    devices = range(lax.axis_size(axis))
    route = [((i - distance) % len(devices), i) for i in devices]
    return lax.ppermute(block, axis, route)


def silu_slope(values):
    sig = jax.nn.sigmoid(values)
    return sig * (1.0 + values * (1.0 - sig))


def on_device(
    grid_latent,
    mesh_latent,
    mesh_cotangent,
    w_grid,
    w_mesh,
    w_out,
    edge_source,
    edge_target,
    edge_count,
):
    grid_nodes = grid_latent.shape[0]
    mesh_nodes = mesh_latent.shape[0]
    slots = edge_source.shape[0]
    lon_count = lax.axis_size("lon")
    lon_index = lax.axis_index("lon")
    band_index = lax.axis_index("band")
    proj_grid = jnp.dot(grid_latent, w_grid, preferred_element_type=jnp.float32).astype(
        jnp.bfloat16
    )
    proj_mesh = jnp.dot(mesh_latent, w_mesh, preferred_element_type=jnp.float32).astype(
        jnp.bfloat16
    )
    east_proj, east_cot = shifted((proj_mesh, mesh_cotangent), "lon", -1)
    table_proj = jnp.concatenate([proj_mesh, east_proj], axis=0)
    table_cot = jnp.concatenate([mesh_cotangent, east_cot], axis=0)
    block = edge_target // mesh_nodes - band_index * lon_count
    offset = (block - lon_index) % lon_count
    local_rows = offset * mesh_nodes + edge_target % mesh_nodes
    alive = jnp.arange(slots, dtype=jnp.int32) < edge_count[0]
    preact = proj_grid[edge_source].astype(jnp.float32) + table_proj[local_rows].astype(jnp.float32)
    activation = jax.nn.silu(preact).astype(jnp.bfloat16)
    edge_cot = jnp.where(alive[:, None], table_cot[local_rows], jnp.zeros((), jnp.bfloat16))
    grad_w_out = lax.dot_general(
        activation, edge_cot, (((0,), (0,)), ((), ())), preferred_element_type=jnp.float32
    )
    grad_act = lax.dot_general(
        edge_cot, w_out, (((1,), (1,)), ((), ())), preferred_element_type=jnp.float32
    )
    grad_pre = (grad_act * silu_slope(preact)).astype(jnp.bfloat16).astype(jnp.float32)
    grad_proj_grid = jax.ops.segment_sum(grad_pre, edge_source, num_segments=grid_nodes).astype(
        jnp.bfloat16
    )
    mesh_terms = jax.ops.segment_sum(grad_pre, local_rows, num_segments=2 * mesh_nodes)
    west_terms = shifted(mesh_terms[mesh_nodes:].astype(jnp.bfloat16), "lon", 1).astype(jnp.float32)
    grad_proj_mesh = (mesh_terms[:mesh_nodes] + west_terms).astype(jnp.bfloat16)
    grid_grad = lax.dot_general(
        grad_proj_grid, w_grid, (((1,), (1,)), ((), ())), preferred_element_type=jnp.float32
    ).astype(jnp.bfloat16)
    mesh_grad = lax.dot_general(
        grad_proj_mesh, w_mesh, (((1,), (1,)), ((), ())), preferred_element_type=jnp.float32
    ).astype(jnp.bfloat16)
    grad_w_grid = lax.dot_general(
        grid_latent, grad_proj_grid, (((0,), (0,)), ((), ())), preferred_element_type=jnp.float32
    )
    grad_w_mesh = lax.dot_general(
        mesh_latent, grad_proj_mesh, (((0,), (0,)), ((), ())), preferred_element_type=jnp.float32
    )
    stacked = jnp.concatenate([grad_w_grid, grad_w_mesh, grad_w_out], axis=0)
    pieces = lax.psum_scatter(stacked, "lon", scatter_dimension=0, tiled=True)
    weight_grads = lax.psum(pieces.astype(jnp.bfloat16), "band").astype(jnp.float32)
    return (grid_grad, mesh_grad, weight_grads)


def solution(mesh):
    in_specs = (
        P(("band", "lon"), None),
        P(("band", "lon"), None),
        P(("band", "lon"), None),
        P(),
        P(),
        P(),
        P(("band", "lon")),
        P(("band", "lon")),
        P(("band", "lon")),
    )
    out_specs = (P(("band", "lon"), None), P(("band", "lon"), None), P("lon", None))
    return jax.shard_map(
        on_device, mesh=mesh, in_specs=in_specs, out_specs=out_specs, check_vma=False
    )
```

profile of v0, /device:TPU:2, one launch (start us, length us, event | category | flops | bytes accessed | tf_op | source)
XLA Modules:
  0.0 348.0 jit_solution(18207047781414758287)
XLA Ops:
  7.2 0.0 reduce-scatter.2.cloned.1.call-start
  7.2 1.4 convolution_convert_fusion.3
  8.7 14.0 %collective-permute-start.1 = (bf16[128,512]{1,0:T(8,128)(2,1)S(1)}, bf16[128,512]{1,0:T(8,128)(2,1)S(1)}, u32[]{:S(2)}, u32[]{:S(2)}) collective-permute-start(bf16[128,512]{1,0:T(8,128)(2,1)S(1)} %convolution_convert_fusion.3), channel_id=1, source_target_pairs={{1,0},{2,1},{3,2},{4,3},{5,4},{6,5},{7,6},{8,7},{9,8},{10,9},{11,1... | collective-permute-start | bytes 393224 | tf_op jit(solution)/shard_map/ppermute | solution.py:10
  22.7 2.6 collective-permute-start
  25.3 1.7 convolution_convert_fusion.1
  27.8 9.2 %gather_fusion.1 = bf16[2048,512]{1,0:T(8,128)(2,1)} fusion(bf16[1024,512]{1,0:T(8,128)(2,1)S(1)} %convolution_convert_fusion.1, s32[2048]{0:T(1024)S(1)} %fusion.16), kind=kCustom, calls=%fused_computation.1 | custom fusion | bytes 4202496 | tf_op jit(solution)/shard_map/gather | solution.py:48
  37.0 9.2 %gather_fusion = bf16[2048,512]{1,0:T(8,128)(2,1)} fusion(bf16[256,512]{1,0:T(8,128)(2,1)S(1)} %pad_maximum_fusion.1, s32[2048]{0:T(1024)S(1)} %get-tuple-element.3), kind=kCustom, calls=%fused_computation | custom fusion | bytes 4202496 | tf_op jit(solution)/shard_map/gather | solution.py:50
  46.3 9.2 %gather_fusion.2 = bf16[2048,512]{1,0:T(8,128)(2,1)} fusion(bf16[256,512]{1,0:T(8,128)(2,1)S(1)} %pad_maximum_fusion.2, s32[2048]{0:T(1024)S(1)} %get-tuple-element.3), kind=kCustom, calls=%fused_computation.2 | custom fusion | bytes 4202496 | tf_op jit(solution)/shard_map/gather | solution.py:48
  55.5 5.2 %fusion.4 = f32[512,512]{1,0:T(8,128)} fusion(bf16[2048,512]{1,0:T(8,128)(2,1)} %gather_fusion.2, bf16[2048,512]{1,0:T(8,128)(2,1)S(1)} %copy-done.3, bf16[2048,512]{1,0:T(8,128)(2,1)} %gather_fusion, pred[2048]{0:T(1024)(128)(4,1)S(1)} %iota_compare_fusion), kind=kOutput, calls=%fused_computation.15 | convolution fusion | flops 1083179008 | bytes 7342080 | tf_op jit(solution)/shard_map/dot_general | solution.py:51
  60.7 3.6 %multiply_convert_fusion.1 = bf16[2048,512]{1,0:T(8,128)(2,1)} fusion(bf16[2048,512]{1,0:T(8,128)(2,1)S(1)} %copy-done.5, bf16[2048,512]{1,0:T(8,128)(2,1)S(1)} %copy-done.3, bf16[512,512]{1,0:T(8,128)(2,1)S(1)} %copy-done.12, bf16[2048,512]{1,0:T(8,128)(2,1)S(1)} %copy-done.4, pred[2048]{0:T(1024)(128)(4,1)S(1)} %iota_compare_fusion), kind=kOutput, calls=%fused_computation.10 | convolution fusion | flops 1087373312 | bytes 8914944 | tf_op jit(solution)/shard_map/dot_general | solution.py:54
  64.3 13.8 %scatter_custom_fusion = f32[1024,512]{1,0:T(8,128)S(1)} fusion(s32[2048]{0:T(1024)S(1)} %copy-done.11, bf16[2048,512]{1,0:T(8,128)(2,1)} %multiply_convert_fusion.1, f32[]{:T(128)} %constant.43.clone.1), kind=kCustom, calls=%fused_computation.7 | custom fusion | flops 2097152 | bytes 4194308 | tf_op jit(solution)/shard_map/scatter-add | solution.py:58
  78.2 14.1 %scatter_custom_fusion.1 = f32[256,512]{1,0:T(8,128)} fusion(s32[2048]{0:T(1024)S(1)} %get-tuple-element.4, bf16[2048,512]{1,0:T(8,128)(2,1)} %multiply_convert_fusion.1, f32[]{:T(128)} %constant.43.clone.1), kind=kCustom, calls=%fused_computation.5 | custom fusion | flops 2097152 | bytes 2621444 | tf_op jit(solution)/shard_map/scatter-add | solution.py:61
  92.3 1.0 slice.23
  93.3 2.1 collective-permute-start.2
  95.3 0.8 convolution_bitcast_fusion.1
  96.1 5.7 %collective-permute-done.2 = bf16[128,512]{1,0:T(8,128)(2,1)S(1)} collective-permute-done((bf16[128,512]{1,0:T(8,128)(2,1)S(1)}, bf16[128,512]{1,0:T(8,128)(2,1)S(1)}, u32[]{:S(2)}, u32[]{:S(2)}) %collective-permute-start.2) | collective-permute-done | bytes 131104 | tf_op jit(solution)/shard_map/ppermute | solution.py:10
  101.8 0.4 convolution_bitcast_fusion
  102.2 1.9 pad_maximum_fusion
  104.2 2.8 convolution_convert_fusion
  107.0 1.0 convolution_convert_fusion.2
  108.0 202.2 %reduce-scatter.2.cloned.1.call-done = f32[16,512]{1,0:T(8,128)} async-done(((f32[1536,512]{1,0:T(8,128)}), f32[16,512]{1,0:T(8,128)}) %reduce-scatter.2.cloned.1.call-update) | async-done | bytes 32784 | tf_op jit(solution)/shard_map/reduce_scatter | solution.py:77
  310.1 0.8 convert_element_type.55
  310.9 29.7 %psum.7 = bf16[16,512]{1,0:T(8,128)(2,1)S(1)} all-reduce(bf16[16,512]{1,0:T(8,128)(2,1)S(1)} %convert_element_type.55), channel_id=1, replica_groups=mesh['band'=8,'lon'=96] {'band'}, use_global_device_ids=true, to_apply=%region_3.4 | all-reduce | flops 8192 | bytes 32768 | tf_op jit(solution)/shard_map/psum | solution.py:78
  340.6 0.6 convert_element_type.56
  (34 shorter events, 0.2 us)
Async XLA Ops:
  7.2 18.1 %copy-start = (bf16[1024,512]{1,0:T(8,128)(2,1)S(1)}, bf16[1024,512]{1,0:T(8,128)(2,1)}, u32[]{:S(2)}) copy-start(bf16[1024,512]{1,0:T(8,128)(2,1)} %param.9) | copy-start | bytes 3145732
  7.2 19.9 %copy-start.10 = (s32[2048]{0:T(1024)S(1)}, s32[2048]{0:T(1024)}, u32[]{:S(2)}) copy-start(s32[2048]{0:T(1024)} %param.16) | copy-start | bytes 24580
  7.2 19.9 %copy-start.11 = (s32[2048]{0:T(1024)S(1)}, s32[2048]{0:T(1024)}, u32[]{:S(2)}) copy-start(s32[2048]{0:T(1024)} %param.15) | copy-start | bytes 24580
  7.2 302.9 %reduce-scatter.2.cloned.1.call-start = ((), (), s32[]{:S(2)}) async-start(), calls=%async_computation.1 | async-start | bytes 3178496 | tf_op jit(solution)/shard_map/reduce_scatter | solution.py:77
  8.7 37.6 %collective-permute-start.1 = (bf16[128,512]{1,0:T(8,128)(2,1)S(1)}, bf16[128,512]{1,0:T(8,128)(2,1)S(1)}, u32[]{:S(2)}, u32[]{:S(2)}) collective-permute-start(bf16[128,512]{1,0:T(8,128)(2,1)S(1)} %convolution_convert_fusion.3), channel_id=1, source_target_pairs={{1,0},{2,1},{3,2},{4,3},{5,4},{6,5},{7,6},{8,7},{9,8},{10,9},{11,1... | collective-permute-start | bytes 393224 | tf_op jit(solution)/shard_map/ppermute | solution.py:10
  22.7 14.3 %collective-permute-start = (bf16[128,512]{1,0:T(8,128)(2,1)}, bf16[128,512]{1,0:T(8,128)(2,1)S(1)}, u32[]{:S(2)}, u32[]{:S(2)}) collective-permute-start(bf16[128,512]{1,0:T(8,128)(2,1)} %param.11), channel_id=1, source_target_pairs={{1,0},{2,1},{3,2},{4,3},{5,4},{6,5},{7,6},{8,7},{9,8},{10,9},{11,1... | collective-permute-start | bytes 393224 | tf_op jit(solution)/shard_map/ppermute | solution.py:10
  27.8 9.2 %copy-start.9 = (bf16[128,512]{1,0:T(8,128)(2,1)S(1)}, bf16[128,512]{1,0:T(8,128)(2,1)}, u32[]{:S(2)}) copy-start(bf16[128,512]{1,0:T(8,128)(2,1)} %param.11) | copy-start | bytes 393220
  46.3 9.2 %copy-start.3 = (bf16[2048,512]{1,0:T(8,128)(2,1)S(1)}, bf16[2048,512]{1,0:T(8,128)(2,1)}, u32[]{:S(2)}) copy-start(bf16[2048,512]{1,0:T(8,128)(2,1)} %gather_fusion.1) | copy-start | bytes 6291460
  55.5 5.2 %copy-start.4 = (bf16[2048,512]{1,0:T(8,128)(2,1)S(1)}, bf16[2048,512]{1,0:T(8,128)(2,1)}, u32[]{:S(2)}) copy-start(bf16[2048,512]{1,0:T(8,128)(2,1)} %gather_fusion) | copy-start | bytes 6291460
  55.5 5.2 %copy-start.5 = (bf16[2048,512]{1,0:T(8,128)(2,1)S(1)}, bf16[2048,512]{1,0:T(8,128)(2,1)}, u32[]{:S(2)}) copy-start(bf16[2048,512]{1,0:T(8,128)(2,1)} %gather_fusion.2) | copy-start | bytes 6291460
  55.5 5.2 %copy-start.12 = (bf16[512,512]{1,0:T(8,128)(2,1)S(1)}, bf16[512,512]{1,0:T(8,128)(2,1)}, u32[]{:S(2)}) copy-start(bf16[512,512]{1,0:T(8,128)(2,1)} %param.14) | copy-start | bytes 1572868
  93.2 8.6 %copy-start.1 = (f32[256,512]{1,0:T(8,128)S(1)}, f32[256,512]{1,0:T(8,128)}, u32[]{:S(2)}) copy-start(f32[256,512]{1,0:T(8,128)} %scatter_custom_fusion.1) | copy-start | bytes 1572868
  93.2 8.6 %copy-start.8 = (bf16[128,512]{1,0:T(8,128)(2,1)S(1)}, bf16[128,512]{1,0:T(8,128)(2,1)}, u32[]{:S(2)}) copy-start(bf16[128,512]{1,0:T(8,128)(2,1)} %param.10) | copy-start | bytes 393220
  93.2 8.9 %copy-start.7 = (f32[512,512]{1,0:T(8,128)S(1)}, f32[512,512]{1,0:T(8,128)}, u32[]{:S(2)}) copy-start(f32[512,512]{1,0:T(8,128)} %fusion.4) | copy-start | bytes 3145732
  93.3 8.5 %collective-permute-start.2 = (bf16[128,512]{1,0:T(8,128)(2,1)S(1)}, bf16[128,512]{1,0:T(8,128)(2,1)S(1)}, u32[]{:S(2)}, u32[]{:S(2)}) collective-permute-start(bf16[128,512]{1,0:T(8,128)(2,1)S(1)} %slice.23), channel_id=1, source_target_pairs={{95,0},{0,1},{1,2},{2,3},{3,4},{4,5},{5,6},{6,7},{7,8},{8,9},{9,10... | collective-permute-start | bytes 393224 | tf_op jit(solution)/shard_map/ppermute | solution.py:10
  104.1 2.9 copy-start.2
  104.1 2.9 copy-start.6
Sparse Core Ops, SparseCore 0:
  104.3 205.8 reduce-scatter.1
where the time goes:
time: 349 us; the launch traced here: 348 us
  waiting for transfers between devices  208 us (60%)
  other arithmetic  31.3 us (9%)
  blocking collectives  29.7 us (9%)
  local copies, waits for them, and re-layouts  28.7 us (8%)
  starting transfers between devices  18.7 us (5%)
  matrix products  16.8 us (5%)
  between operations  14.9 us (4%)
    reduce_scatter x1, waiting for transfers between devices, on_device(): pieces = lax.psum_scatter(stacked, 'lon', scatter_dimension=0, tiled=True)  202 us
    psum x1, blocking collectives, on_device(): lax.psum(pieces.astype(jnp.bfloat16), 'band').astype(jnp.float32)  29.7 us
    ppermute x3, starting transfers between devices, shifted(): return lax.ppermute(block, axis, route)  18.6 us
    scatter-add x1, other arithmetic, on_device(): jax.ops.segment_sum(grad_pre, local_rows, num_segments=2 * mesh_nodes)  14.1 us
    scatter-add x1, other arithmetic, on_device(): jax.ops.segment_sum(grad_pre, edge_source, num_segments=grid_nodes)  13.8 us
    gather x1, local copies, waits for them, and re-layouts, on_device(): table_cot[local_rows]  9.24 us
    gather x1, local copies, waits for them, and re-layouts, on_device(): table_proj[local_rows].astype(jnp.float32)  9.22 us
    gather x1, local copies, waits for them, and re-layouts, on_device(): proj_grid[edge_source].astype(jnp.float32)  9.21 us
  transfers between devices with their start and end apart: 4, of which 2 were waited for; matrix products, arithmetic and copies ran while one was open for 7% of the time, Pallas kernels for 0%

commit v1 on v0

v1 whole, which is shorter than its diff:
```python
import jax
import jax.numpy as jnp
from jax import lax
from jax.experimental import pallas as pl
from jax.experimental.pallas import tpu as pltpu
from jax.sharding import PartitionSpec as P

MESH = pl.DeviceIdType.MESH
BF16 = jnp.bfloat16
F32 = jnp.float32

D = 512
HALF = 256
GRID_ROWS = 1024
MESH_ROWS = 128
TABLE = 2 * MESH_ROWS
SLOTS = 2048
LANES = 128
NX, NY, NZ, NC = 4, 8, 12, 2
N_LON = NX * NZ * NC
GRID_TYPE, MESH_TYPE, OUT_TYPE = 0, 1, 2


def dot(a, b):
    return lax.dot_general(a, b, (((1,), (0,)), ((), ())), preferred_element_type=F32)


def dot_bt(a, b):
    return lax.dot_general(a, b, (((1,), (1,)), ((), ())), preferred_element_type=F32)


def lon_of(x, z, c):
    return (x * NZ + z) * NC + c


def piece_rows(kind, c, x):
    if kind == GRID_TYPE:
        return ((1 - c) * NX + x) * 64
    if kind == MESH_TYPE:
        return (c * NX + x) * 64
    return c * HALF + ((x + 1) % NX) * 64


def owner_of(x, z, c, half):
    kind, j = z // 4, z % 4
    grid = (1 - c) * 16 + x * 4 + j
    mesh = 32 + c * 16 + x * 4 + j
    out = 64 + 16 * half + 4 * ((x + 1) % NX) + j
    return jnp.where(kind == 0, grid, jnp.where(kind == 1, mesh, out))


def summer_of(lon, which):
    kind = lon // 32
    k = lon % 32
    grid = lon_of((k // 4) % NX, k % 4, 1 - k // 16)
    mesh = lon_of((k // 4) % NX, 4 + k % 4, k // 16)
    b = lon % 16
    out = lon_of((b // 4 + 3) % NX, 8 + b % 4, which)
    return jnp.where(kind == 0, grid, jnp.where(kind == 1, mesh, out))


def kernel(
    gl_hbm, ml_hbm, ct_hbm, wg_hbm, wm_hbm, wo_hbm, src_hbm, tgt_hbm, cnt_hbm,
    gg_hbm, mg_hbm, wgrad_hbm,
    gl, glt, wg, wm, wo, ml, mlt, ct, src, tgt, cnt,
    pick, pickt, table, gtable, actgp, gpg, gg, mg,
    mine, tosend, west,
    piece, core_in, mid, x_in, low, z_in, last, y_in, wout,
    load_sem, store_sem,
    east_send, east_recv, west_send, west_recv,
    core_send, core_recv, x_send, x_recv, z_send, z_recv, y_send, y_recv,
):
    band = lax.axis_index("band")
    lon = lax.axis_index("lon")
    x = lon // (NZ * NC)
    z = (lon // NC) % NZ
    c = lon % NC
    kind = z // 4
    own_kind = lon // 32
    to_west = (band, (lon + N_LON - 1) % N_LON)
    to_east = (band, (lon + 1) % N_LON)
    mate = (band, lon_of(x, z, 1 - c))

    def load(i, source, target):
        return pltpu.make_async_copy(source, target, load_sem.at[i])

    loads = [
        load(0, ml_hbm, ml.at[pl.ds(0, MESH_ROWS)]),
        load(1, ct_hbm, ct.at[pl.ds(0, MESH_ROWS)]),
        load(2, src_hbm, src),
        load(3, tgt_hbm, tgt),
        load(4, cnt_hbm, cnt),
        load(5, gl_hbm, gl),
        load(6, wg_hbm, wg),
        load(7, wm_hbm, wm),
        load(8, wo_hbm, wo),
    ]
    for copy in loads:
        copy.start()

    barrier = pltpu.get_barrier_semaphore()

    def greet(device):
        pl.semaphore_signal(barrier, inc=1, device_id=device, device_id_type=MESH)

    greet(to_west)
    greet(to_east)
    greet(mate)
    for d in range(1, NX):
        greet((band, lon_of((x + d) % NX, z, c)))

    def greet_z(d, carry):
        greet((band, lon_of(x, (z + d) % NZ, c)))
        return carry

    lax.fori_loop(1, NZ, greet_z, 0)

    def greet_y(y, carry):
        greet((y, owner_of(x, z, c, 0)))
        greet((y, summer_of(lon, 0)))

        @pl.when(kind == OUT_TYPE)
        def _():
            greet((y, owner_of(x, z, c, 1)))

        @pl.when(own_kind == OUT_TYPE)
        def _():
            greet((y, summer_of(lon, 1)))

        return carry

    lax.fori_loop(0, NY, greet_y, 0)
    loads[0].wait()
    loads[1].wait()
    pl.semaphore_wait(
        barrier,
        3 + (NX - 1) + (NZ - 1) + 2 * NY
        + jnp.where(kind == OUT_TYPE, NY, 0) + jnp.where(own_kind == OUT_TYPE, NY, 0),
    )

    def east_copy(i, ref):
        return pltpu.make_async_remote_copy(
            src_ref=ref.at[pl.ds(0, MESH_ROWS)],
            dst_ref=ref.at[pl.ds(MESH_ROWS, MESH_ROWS)],
            send_sem=east_send.at[i],
            recv_sem=east_recv.at[i],
            device_id=to_west,
            device_id_type=MESH,
        )

    def west_copy(half):
        return pltpu.make_async_remote_copy(
            src_ref=tosend.at[half],
            dst_ref=west.at[half],
            send_sem=west_send.at[half],
            recv_sem=west_recv.at[half],
            device_id=to_east,
            device_id_type=MESH,
        )

    def core_copy(half, t):
        return pltpu.make_async_remote_copy(
            src_ref=piece.at[half, t, 1 - c],
            dst_ref=core_in.at[half, t],
            send_sem=core_send.at[half, t],
            recv_sem=core_recv.at[half, t],
            device_id=mate,
            device_id_type=MESH,
        )

    def x_copy(half, t, d):
        there = (x + d) % NX
        return pltpu.make_async_remote_copy(
            src_ref=mid.at[half, t, there],
            dst_ref=x_in.at[half, t, d - 1],
            send_sem=x_send.at[half, t, d - 1],
            recv_sem=x_recv.at[half, t, d - 1],
            device_id=(band, lon_of(there, z, c)),
            device_id_type=MESH,
        )

    def z_copy(half, there):
        slot = (there + NZ - z + NZ - 1) % NZ
        return pltpu.make_async_remote_copy(
            src_ref=low.at[half, there],
            dst_ref=z_in.at[half, slot],
            send_sem=z_send.at[half],
            recv_sem=z_recv.at[half],
            device_id=(band, lon_of(x, there, c)),
            device_id_type=MESH,
        )

    def y_copy(half, y):
        side = jnp.where(kind == OUT_TYPE, c, half)
        return pltpu.make_async_remote_copy(
            src_ref=last.at[half],
            dst_ref=y_in.at[side, band],
            send_sem=y_send.at[half],
            recv_sem=y_recv.at[side],
            device_id=(y, owner_of(x, z, c, half)),
            device_id_type=MESH,
        )

    def whole(ref, send, recv):
        return pltpu.make_async_remote_copy(
            src_ref=ref, dst_ref=ref, send_sem=send, recv_sem=recv,
            device_id=mate, device_id_type=MESH,
        )

    east_copy(0, ml).start()
    east_copy(1, ct).start()

    for i in (2, 3, 4):
        loads[i].wait()

    slot = lax.broadcasted_iota(jnp.int32, (SLOTS // LANES, LANES), 0) * LANES
    slot = slot + lax.broadcasted_iota(jnp.int32, (SLOTS // LANES, LANES), 1)
    target = tgt[...]
    start = (band * N_LON + lon) * MESH_ROWS
    here = (target >= start) & (target < start + MESH_ROWS)
    row = jnp.where(here, target - start, MESH_ROWS + (target & (MESH_ROWS - 1)))
    alive = slot < cnt[...]
    tgt[...] = jnp.where(alive, row, -1) + GRID_ROWS

    def build(r, carry):
        s = src[pl.ds(r, 1), :]
        t = tgt[pl.ds(r, 1), :]
        columns = pl.ds(pl.multiple_of(r * LANES, LANES), LANES)
        down = lax.broadcasted_iota(jnp.int32, (LANES, LANES), 0)
        across = lax.broadcasted_iota(jnp.int32, (LANES, LANES), 1)
        sb = jnp.broadcast_to(s, (LANES, LANES))
        tb = jnp.broadcast_to(jnp.where(t < GRID_ROWS, -1, t), (LANES, LANES))
        st = sb.T
        tt = tb.T
        for k in range((GRID_ROWS + TABLE) // LANES):
            one = (sb if k < GRID_ROWS // LANES else tb) == down + k * LANES
            pickt[k * LANES:(k + 1) * LANES, columns] = jnp.where(one, 1.0, 0.0).astype(BF16)
            one = (st if k < GRID_ROWS // LANES else tt) == across + k * LANES
            pick[columns, k * LANES:(k + 1) * LANES] = jnp.where(one, 1.0, 0.0).astype(BF16)
        return carry

    lax.fori_loop(0, SLOTS // LANES, build, 0)

    loads[5].wait()
    loads[6].wait()

    def turn(i, carry):
        rows = pl.ds(pl.multiple_of(i * 256, 256), 256)
        glt[:, rows] = gl[rows, :].T
        return carry

    lax.fori_loop(0, GRID_ROWS // 256, turn, 0)

    def put(half, t, values):
        values = values.astype(BF16)
        for cc in range(NC):
            for xx in range(NX):
                first = piece_rows(t, cc, xx)
                piece[half, t, cc, xx] = values[first:first + 64]
        core_copy(half, t).start()

    def after_core(half, t):
        core_copy(half, t).wait_recv()
        for xx in range(NX):
            total = piece[half, t, c, xx].astype(F32) + core_in[half, t, xx].astype(F32)
            mid[half, t, xx] = total.astype(BF16)
        for d in range(1, NX):
            x_copy(half, t, d).start()

    def after_x(half, t):
        for d in range(1, NX):
            x_copy(half, t, d).wait_recv()
        total = mid[half, t, x].astype(F32)
        for d in range(1, NX):
            total = total + x_in[half, t, d - 1].astype(F32)
        total = total.astype(BF16)
        for j in range(4):
            low[half, t * 4 + j] = total[j * 16:(j + 1) * 16]
        for j in range(4):
            @pl.when(z != t * 4 + j)
            def _():
                z_copy(half, t * 4 + j).start()

    def after_z(half):
        whole(z_in.at[half], z_send.at[half], z_recv.at[half]).wait_recv()
        total = low[half, z].astype(F32)
        for s in range(NZ - 1):
            total = total + z_in[half, s].astype(F32)
        last[half] = total.astype(BF16)

        def send(y, carry):
            y_copy(half, y).start()
            return carry

        lax.fori_loop(0, NY, send, 0)

    def tables(half):
        columns = slice(half * HALF, (half + 1) * HALF)

        def project(i, carry):
            rows = pl.ds(pl.multiple_of(i * 256, 256), 256)
            table[rows, :] = dot(gl[rows, :], wg[:, columns]).astype(BF16)
            return carry

        lax.fori_loop(0, GRID_ROWS // 256, project, 0)
        if half == 0:
            loads[7].wait()
            loads[8].wait()
            east_copy(0, ml).wait_recv()
            east_copy(1, ct).wait_recv()
            mlt[...] = ml[...].T
        table[GRID_ROWS:, :] = dot(ml[...], wm[:, columns]).astype(BF16)
        gtable[...] = dot_bt(ct[...], wo[columns, :]).astype(BF16)

    def edges(half):
        def step(i, carry):
            rows = pl.ds(pl.multiple_of(i * 256, 256), 256)
            pre = dot(pick[rows, :], table[...])
            grad = dot(pick[rows, GRID_ROWS:], gtable[...])
            sig = 0.5 * jnp.tanh(0.5 * pre) + 0.5
            act = pre * sig
            actgp[rows, :HALF] = act.astype(BF16)
            actgp[rows, HALF:] = (grad * (sig + act * (1.0 - sig))).astype(BF16)
            return carry

        lax.fori_loop(0, SLOTS // 256, step, 0)

    def mesh_side(half):
        sums = dot(pickt[GRID_ROWS:, :], actgp[...])
        terms = sums[:, HALF:]
        mine[half] = terms[:MESH_ROWS]
        termsb = terms.astype(BF16)
        tosend[half] = termsb[MESH_ROWS:]
        west_copy(half).start()
        acts = sums[:, :HALF].T.astype(BF16)
        out = dot(acts, ct[...])
        put(half, OUT_TYPE, jnp.concatenate([out[:, :HALF], out[:, HALF:]], axis=0))
        put(half, MESH_TYPE, dot(mlt[...], termsb))

    def grid_side(half):
        columns = slice(half * HALF, (half + 1) * HALF)

        def step(i, carry):
            rows = pl.ds(pl.multiple_of(i * 256, 256), 256)
            gpg[rows, columns] = dot(pickt[rows, :], actgp[:, HALF:]).astype(BF16)
            return carry

        lax.fori_loop(0, GRID_ROWS // 256, step, 0)

    def grid_weights(half):
        columns = slice(half * HALF, (half + 1) * HALF)
        put(half, GRID_TYPE, dot(glt[...], gpg[:, columns]))

    def grid_grads(first):
        def step(i, carry):
            rows = pl.ds(pl.multiple_of(i * 256, 256), 256)
            gg[rows, :] = dot_bt(gpg[rows, :], wg[...]).astype(BF16)
            return carry

        lax.fori_loop(first, first + 2, step, 0)

    def store(i, source, goal):
        return pltpu.make_async_copy(source, goal, store_sem.at[i])

    tables(0)
    edges(0)
    mesh_side(0)
    grid_side(0)
    grid_weights(0)
    tables(1)
    for t in (OUT_TYPE, MESH_TYPE, GRID_TYPE):
        after_core(0, t)
    edges(1)
    for t in (OUT_TYPE, MESH_TYPE, GRID_TYPE):
        after_x(0, t)
    mesh_side(1)
    grid_side(1)
    after_core(1, OUT_TYPE)
    after_core(1, MESH_TYPE)
    grid_weights(1)
    after_z(0)
    after_x(1, OUT_TYPE)
    after_x(1, MESH_TYPE)
    after_core(1, GRID_TYPE)
    grid_grads(0)
    after_x(1, GRID_TYPE)
    grid_grads(2)
    store(0, gg, gg_hbm).start()
    for half in range(2):
        west_copy(half).wait_recv()
    total = jnp.zeros((MESH_ROWS, D), F32)
    for half in range(2):
        columns = slice(half * HALF, (half + 1) * HALF)
        sums = (mine[half] + west[half].astype(F32)).astype(BF16)
        total = total + dot_bt(sums, wm[:, columns])
    mg[...] = total.astype(BF16)
    store(1, mg, mg_hbm).start()
    after_z(1)
    for side in range(2):
        whole(y_in.at[side], y_send.at[side], y_recv.at[side]).wait_recv()
        total = y_in[side, 0].astype(F32)
        for s in range(1, NY):
            total = total + y_in[side, s].astype(F32)
        wout[:, side * HALF:(side + 1) * HALF] = total
    store(2, wout, wgrad_hbm).start()

    east_copy(0, ml).wait_send()
    east_copy(1, ct).wait_send()
    for half in range(2):
        west_copy(half).wait_send()
        for t in range(3):
            core_copy(half, t).wait_send()
            for d in range(1, NX):
                x_copy(half, t, d).wait_send()
        whole(z_in.at[half], z_send.at[half], z_recv.at[half]).wait_send()
        whole(y_in.at[half], y_send.at[half], y_recv.at[half]).wait_send()
    store(0, gg, gg_hbm).wait()
    store(1, mg, mg_hbm).wait()
    store(2, wout, wgrad_hbm).wait()


def on_device(
    grid_latent, mesh_latent, mesh_cotangent, w_grid, w_mesh, w_out, edge_source, edge_target, edge_count
):
    edges = (SLOTS // LANES, LANES)
    count = jnp.broadcast_to(edge_count.reshape(1, 1), edges)
    dma = pltpu.SemaphoreType.DMA
    vmem = pltpu.VMEM
    return pl.pallas_call(
        kernel,
        out_shape=(
            jax.ShapeDtypeStruct((GRID_ROWS, D), BF16),
            jax.ShapeDtypeStruct((MESH_ROWS, D), BF16),
            jax.ShapeDtypeStruct((16, D), F32),
        ),
        in_specs=[pl.BlockSpec(memory_space=pl.ANY)] * 9,
        out_specs=[pl.BlockSpec(memory_space=pl.ANY)] * 3,
        scratch_shapes=[
            vmem((GRID_ROWS, D), BF16),
            vmem((D, GRID_ROWS), BF16),
            vmem((D, D), BF16),
            vmem((D, D), BF16),
            vmem((D, D), BF16),
            vmem((TABLE, D), BF16),
            vmem((D, TABLE), BF16),
            vmem((TABLE, D), BF16),
            vmem(edges, jnp.int32),
            vmem(edges, jnp.int32),
            vmem(edges, jnp.int32),
            vmem((SLOTS, GRID_ROWS + TABLE), BF16),
            vmem((GRID_ROWS + TABLE, SLOTS), BF16),
            vmem((GRID_ROWS + TABLE, HALF), BF16),
            vmem((TABLE, HALF), BF16),
            vmem((SLOTS, D), BF16),
            vmem((GRID_ROWS, D), BF16),
            vmem((GRID_ROWS, D), BF16),
            vmem((MESH_ROWS, D), BF16),
            vmem((2, MESH_ROWS, HALF), F32),
            vmem((2, MESH_ROWS, HALF), BF16),
            vmem((2, MESH_ROWS, HALF), BF16),
            vmem((2, 3, NC, NX, 64, HALF), BF16),
            vmem((2, 3, NX, 64, HALF), BF16),
            vmem((2, 3, NX, 64, HALF), BF16),
            vmem((2, 3, NX - 1, 64, HALF), BF16),
            vmem((2, NZ, 16, HALF), BF16),
            vmem((2, NZ - 1, 16, HALF), BF16),
            vmem((2, 16, HALF), BF16),
            vmem((2, NY, 16, HALF), BF16),
            vmem((16, D), F32),
            dma((9,)),
            dma((3,)),
            dma((2,)),
            dma((2,)),
            dma((2,)),
            dma((2,)),
            dma((2, 3)),
            dma((2, 3)),
            dma((2, 3, NX - 1)),
            dma((2, 3, NX - 1)),
            dma((2,)),
            dma((2,)),
            dma((2,)),
            dma((2,)),
        ],
        compiler_params=pltpu.CompilerParams(
            collective_id=0, has_side_effects=True, vmem_limit_bytes=56 * 1024 * 1024
        ),
        cost_estimate=pl.CostEstimate(flops=17_000_000_000, bytes_accessed=5_000_000, transcendentals=1_000_000),
    )(
        grid_latent, mesh_latent, mesh_cotangent, w_grid, w_mesh, w_out,
        edge_source.reshape(edges), edge_target.reshape(edges), count,
    )


def solution(mesh):
    in_specs = (
        P(("band", "lon"), None),
        P(("band", "lon"), None),
        P(("band", "lon"), None),
        P(),
        P(),
        P(),
        P(("band", "lon")),
        P(("band", "lon")),
        P(("band", "lon")),
    )
    out_specs = (P(("band", "lon"), None), P(("band", "lon"), None), P("lon", None))
    return jax.shard_map(
        on_device, mesh=mesh, in_specs=in_specs, out_specs=out_specs, check_vma=False
    )
```

time: 349 us -> 70.7 us (0.20)
  the two profiles are of different devices: /device:TPU:2 before, /device:TPU:10 now
where the time goes in v1:
time: 70.7 us; the launch traced here: 70.5 us
  Pallas kernels  64.9 us (92%)
  local copies, waits for them, and re-layouts  4.27 us (6%)
  between operations  1.3 us (2%)
    pallas_call x1, Pallas kernels, on_device(): pl.pallas_call(kernel, out_shape=(jax.ShapeDtypeStruct((GRID_ROWS, D), BF...  64.9 us
    unnamed x7, local copies, waits for them, and re-layouts  3.67 us

profile of v1, /device:TPU:10, one launch (start us, length us, event | category | flops | bytes accessed | tf_op | source)
XLA Modules:
  0.0 70.5 jit_solution(18271865243567914402)
XLA Ops:
  1.3 0.6 broadcast_in_dim.8.cnt_hbm
  1.9 64.9 %shard_map.112 = (bf16[1024,512]{1,0:T(8,128)(2,1)}, bf16[128,512]{1,0:T(8,128)(2,1)}, f32[16,512]{1,0:T(8,128)}) custom-call(bf16[1024,512]{1,0:T(8,128)(2,1)} %gl_hbm.1, bf16[128,512]{1,0:T(8,128)(2,1)} %ml_hbm.1, bf16[128,512]{1,0:T(8,128)(2,1)} %ct_hbm.1, bf16[512,512]{1,0:T(8,128)(2,1)} %wg_hbm.1, bf16[512,512]{1,0:T(8,128)(2,1)} %wm_hbm.1, ...), custom_call_target="tpu_custom_call" | custom-call | flops 16999999488 | bytes 5000000 | tf_op jit(solution)/shard_map/pallas_call | solution.py:429
  66.8 0.0 copy-start
  66.8 2.3 %copy.16 = bf16[1024,512]{1,0:T(8,128)(2,1)} copy(bf16[1024,512]{1,0:T(8,128)(2,1)} %get-tuple-element.6) | data formatting | bytes 2097152
  69.1 0.0 copy-done
  69.1 0.0 copy-start.1
  69.1 0.7 copy.17
  69.7 0.1 copy-done.1
  69.8 0.6 copy.18
Async XLA Ops:
  66.8 2.3 %copy-start = (bf16[128,512]{1,0:T(8,128)(2,1)S(1)}, bf16[128,512]{1,0:T(8,128)(2,1)}, u32[]{:S(2)}) copy-start(bf16[128,512]{1,0:T(8,128)(2,1)} %get-tuple-element.7) | copy-start | bytes 393220
  69.1 0.8 %copy-start.1 = (f32[16,512]{1,0:T(8,128)S(1)}, f32[16,512]{1,0:T(8,128)}, u32[]{:S(2)}) copy-start(f32[16,512]{1,0:T(8,128)} %get-tuple-element.8) | copy-start | bytes 98308

commit v2 on v0

v2 whole, which is shorter than its diff:
```python
import jax
import jax.numpy as jnp
from jax import lax
from jax.experimental import pallas as pl
from jax.experimental.pallas import tpu as pltpu
from jax.sharding import PartitionSpec as P

MESH = pl.DeviceIdType.MESH
BF16 = jnp.bfloat16
F32 = jnp.float32

D = 512
GRID_ROWS = 1024
MESH_ROWS = 128
TABLE = 2 * MESH_ROWS
SLOTS = 2048
LANES = 128
NX, NY, NZ, NC = 4, 8, 12, 2
N_LON = NX * NZ * NC
GRID_TYPE, MESH_TYPE, OUT_TYPE = 0, 1, 2
SPOTS = (
    ((0, 0), (0, 1), (0, 2), (1, 0)),
    ((1, 1), (1, 2), (2, 0), (2, 1)),
    ((2, 2), (3, 0), (3, 1), (3, 2)),
)


def dot(a, b):
    return lax.dot_general(a, b, (((1,), (0,)), ((), ())), preferred_element_type=F32)


def dot_bt(a, b):
    return lax.dot_general(a, b, (((1,), (1,)), ((), ())), preferred_element_type=F32)


def lon_of(x, z, c):
    return (x * NZ + z) * NC + c


def spot_z(x, t, j):
    owner_x, group = SPOTS[t][j]
    return 4 * group + (x + NX - owner_x) % NX


def block_row(t, c, x, j):
    return 16 * (lon_of(SPOTS[t][j][0], spot_z(x, t, j), c) - 32 * t)


def kernel(
    gl_hbm, ml_hbm, ct_hbm, wg_hbm, wm_hbm, wo_hbm, src_hbm, tgt_hbm, cnt,
    gg_hbm, mg_hbm, wgrad_hbm,
    gl, glt, wg, wm, wo, ml, mlt, ct, src, tgt,
    pick, pickt, table, mtable, pre, actgp, gpg, gg, mg,
    mine, tosend, west,
    piece, core_in, mid, x_in, low, z_in, last, y_in, wout,
    load_sem, store_sem,
    east_send, east_recv, west_send, west_recv,
    core_send, core_recv, x_send, x_recv, z_send, z_recv, y_send, y_recv,
):
    band = lax.axis_index("band")
    lon = lax.axis_index("lon")
    x = lon // (NZ * NC)
    z = (lon // NC) % NZ
    c = lon % NC
    moved = z % NX != 0
    owner = lon_of((x + NZ - z) % NX, z, c)
    summer = lon_of((x + z) % NX, z, c)
    to_west = (band, (lon + N_LON - 1) % N_LON)
    to_east = (band, (lon + 1) % N_LON)
    mate = (band, lon_of(x, z, 1 - c))

    def load(i, source, target):
        return pltpu.make_async_copy(source, target, load_sem.at[i])

    loads = [
        load(0, src_hbm, src),
        load(1, tgt_hbm, tgt),
        load(2, gl_hbm, gl),
        load(3, wg_hbm, wg),
        load(4, ml_hbm, ml.at[pl.ds(0, MESH_ROWS)]),
        load(5, ct_hbm, ct.at[pl.ds(0, MESH_ROWS)]),
        load(6, wm_hbm, wm),
        load(7, wo_hbm, wo),
    ]
    for copy in loads:
        copy.start()

    barrier = pltpu.get_barrier_semaphore()

    def greet(device):
        pl.semaphore_signal(barrier, inc=1, device_id=device, device_id_type=MESH)

    greet(to_west)
    greet(to_east)
    greet(mate)
    for d in range(1, NX):
        greet((band, lon_of((x + d) % NX, z, c)))

    def greet_z(d, carry):
        greet((band, lon_of(x, (z + d) % NZ, c)))
        return carry

    lax.fori_loop(1, NZ, greet_z, 0)

    def greet_y(d, carry):
        greet(((band + d) % NY, owner))
        greet(((band + d) % NY, summer))
        return carry

    lax.fori_loop(1, NY, greet_y, 0)

    @pl.when(moved)
    def _():
        greet((band, owner))
        greet((band, summer))

    def east_copy(i, ref):
        return pltpu.make_async_remote_copy(
            src_ref=ref.at[pl.ds(0, MESH_ROWS)],
            dst_ref=ref.at[pl.ds(MESH_ROWS, MESH_ROWS)],
            send_sem=east_send.at[i],
            recv_sem=east_recv.at[i],
            device_id=to_west,
            device_id_type=MESH,
        )

    def west_copy():
        return pltpu.make_async_remote_copy(
            src_ref=tosend,
            dst_ref=west,
            send_sem=west_send,
            recv_sem=west_recv,
            device_id=to_east,
            device_id_type=MESH,
        )

    def core_copy(t):
        return pltpu.make_async_remote_copy(
            src_ref=piece.at[t, 1 - c],
            dst_ref=core_in.at[t],
            send_sem=core_send.at[t],
            recv_sem=core_recv.at[t],
            device_id=mate,
            device_id_type=MESH,
        )

    def x_copy(t, d):
        there = (x + d) % NX
        return pltpu.make_async_remote_copy(
            src_ref=mid.at[t, there],
            dst_ref=x_in.at[t, d - 1],
            send_sem=x_send.at[t, d - 1],
            recv_sem=x_recv.at[t, d - 1],
            device_id=(band, lon_of(there, z, c)),
            device_id_type=MESH,
        )

    def z_copy(there):
        slot = (there + NZ - z + NZ - 1) % NZ
        return pltpu.make_async_remote_copy(
            src_ref=low.at[there],
            dst_ref=z_in.at[slot],
            send_sem=z_send,
            recv_sem=z_recv,
            device_id=(band, lon_of(x, there, c)),
            device_id_type=MESH,
        )

    def y_copy(y, i):
        return pltpu.make_async_remote_copy(
            src_ref=last,
            dst_ref=y_in.at[band],
            send_sem=y_send.at[i],
            recv_sem=y_recv.at[i],
            device_id=(y, owner),
            device_id_type=MESH,
        )

    def whole(ref, send, recv):
        return pltpu.make_async_remote_copy(
            src_ref=ref, dst_ref=ref, send_sem=send, recv_sem=recv,
            device_id=mate, device_id_type=MESH,
        )

    loads[0].wait()
    loads[1].wait()
    slot = lax.broadcasted_iota(jnp.int32, (SLOTS // LANES, LANES), 0) * LANES
    slot = slot + lax.broadcasted_iota(jnp.int32, (SLOTS // LANES, LANES), 1)
    target = tgt[...]
    start = (band * N_LON + lon) * MESH_ROWS
    here = (target >= start) & (target < start + MESH_ROWS)
    row = jnp.where(here, target - start, MESH_ROWS + (target & (MESH_ROWS - 1)))
    tgt[...] = jnp.where(slot < cnt[0], row + GRID_ROWS, -1)

    def build(r, carry):
        columns = pl.ds(pl.multiple_of(r * LANES, LANES), LANES)
        down = lax.broadcasted_iota(jnp.int32, (LANES, LANES), 0).astype(jnp.int16)
        across = lax.broadcasted_iota(jnp.int32, (LANES, LANES), 1).astype(jnp.int16)
        sb = jnp.broadcast_to(src[pl.ds(r, 1), :], (LANES, LANES)).astype(jnp.int16)
        tb = jnp.broadcast_to(tgt[pl.ds(r, 1), :], (LANES, LANES)).astype(jnp.int16)
        st = sb.T
        tt = tb.T
        for k in range((GRID_ROWS + TABLE) // LANES):
            one = (sb if k < GRID_ROWS // LANES else tb) == down + jnp.int16(k * LANES)
            pickt[k * LANES:(k + 1) * LANES, columns] = jnp.where(one, jnp.ones((), BF16), jnp.zeros((), BF16))
            one = (st if k < GRID_ROWS // LANES else tt) == across + jnp.int16(k * LANES)
            pick[columns, k * LANES:(k + 1) * LANES] = jnp.where(one, jnp.ones((), BF16), jnp.zeros((), BF16))
        return carry

    lax.fori_loop(0, SLOTS // LANES, build, 0)

    loads[2].wait()
    loads[3].wait()

    table[...] = dot(gl[...], wg[...]).astype(BF16)

    for i in range(4, 8):
        loads[i].wait()
    pl.semaphore_wait(barrier, 3 + (NX - 1) + (NZ - 1) + 2 * (NY - 1) + jnp.where(moved, 2, 0))
    east_copy(0, ml).start()
    east_copy(1, ct).start()

    def gather(i, carry):
        rows = pl.ds(pl.multiple_of(i * 1024, 1024), 1024)
        pre[rows, :] = dot(pick[rows, :GRID_ROWS], table[...])
        return carry

    lax.fori_loop(0, SLOTS // 1024, gather, 0)

    def turn(i, carry):
        rows = pl.ds(pl.multiple_of(i * 256, 256), 256)
        glt[:, rows] = gl[rows, :].T
        return carry

    lax.fori_loop(0, GRID_ROWS // 256, turn, 0)

    east_copy(0, ml).wait_recv()
    east_copy(1, ct).wait_recv()
    mlt[...] = ml[...].T
    mtable[:, :D] = dot(ml[...], wm[...]).astype(BF16)
    mtable[:, D:] = dot_bt(ct[...], wo[...]).astype(BF16)

    def edge(i, carry):
        rows = pl.ds(pl.multiple_of(i * 1024, 1024), 1024)
        both = dot(pick[rows, GRID_ROWS:], mtable[...])
        value = pre[rows, :] + both[:, :D]
        sig = 0.5 * jnp.tanh(0.5 * value) + 0.5
        act = value * sig
        actgp[rows, :D] = act.astype(BF16)
        actgp[rows, D:] = (both[:, D:] * (sig + act * (1.0 - sig))).astype(BF16)
        return carry

    lax.fori_loop(0, SLOTS // 1024, edge, 0)

    def put(t, values):
        values = values.astype(BF16)
        for cc in range(NC):
            for xx in range(NX):
                for j in range(4):
                    first = block_row(t, cc, xx, j)
                    piece[t, cc, xx, 16 * j:16 * (j + 1)] = values[first:first + 16]
        core_copy(t).start()

    def after_core(t):
        core_copy(t).wait_recv()
        for xx in range(NX):
            total = piece[t, c, xx].astype(F32) + core_in[t, xx].astype(F32)
            mid[t, xx] = total.astype(BF16)
        for d in (2, 1, 3):
            x_copy(t, d).start()

    def after_x(t):
        for d in range(1, NX):
            x_copy(t, d).wait_recv()
        total = mid[t, x].astype(F32)
        for d in range(1, NX):
            total = total + x_in[t, d - 1].astype(F32)
        total = total.astype(BF16)
        for j in range(4):
            low[spot_z(x, t, j)] = total[16 * j:16 * (j + 1)]
        for j in range(4):
            @pl.when(z != spot_z(x, t, j))
            def _():
                z_copy(spot_z(x, t, j)).start()

    sums = dot(pickt[GRID_ROWS:, :], actgp[...])
    mine[...] = sums[:MESH_ROWS, D:]
    terms = sums[:, D:].astype(BF16)
    tosend[...] = terms[MESH_ROWS:]
    west_copy().start()
    put(OUT_TYPE, dot(sums[:, :D].T.astype(BF16), ct[...]))
    put(MESH_TYPE, dot(mlt[...], terms))

    def grid_side(first):
        def step(i, carry):
            rows = pl.ds(pl.multiple_of(i * 512, 512), 512)
            gpg[rows, :] = dot(pickt[rows, :], actgp[:, D:]).astype(BF16)
            return carry

        lax.fori_loop(first, first + 1, step, 0)

    grid_side(0)
    after_core(OUT_TYPE)
    after_core(MESH_TYPE)
    grid_side(1)
    put(GRID_TYPE, dot(glt[...], gpg[...]))

    def grid_grads(first):
        def step(i, carry):
            rows = pl.ds(pl.multiple_of(i * 512, 512), 512)
            gg[rows, :] = dot_bt(gpg[rows, :], wg[...]).astype(BF16)
            return carry

        lax.fori_loop(first, first + 1, step, 0)

    def store(i, source, goal):
        return pltpu.make_async_copy(source, goal, store_sem.at[i])

    grid_grads(0)
    after_core(GRID_TYPE)
    after_x(OUT_TYPE)
    after_x(MESH_TYPE)
    grid_grads(1)
    store(0, gg, gg_hbm).start()
    west_copy().wait_recv()
    mg[...] = dot_bt((mine[...] + west[...].astype(F32)).astype(BF16), wm[...]).astype(BF16)
    store(1, mg, mg_hbm).start()
    after_x(GRID_TYPE)

    whole(z_in, z_send, z_recv).wait_recv()
    total = low[z].astype(F32)
    for s in range(NZ - 1):
        total = total + z_in[s].astype(F32)
    last[...] = total.astype(BF16)

    for d in (4, 3, 5, 2, 6, 1, 7):
        y_copy((band + d) % NY, 0).start()

    @pl.when(moved)
    def _():
        y_copy(band, 1).start()

    @pl.when(jnp.logical_not(moved))
    def _():
        y_in[band] = last[...]

    rest = y_in.at[pl.ds(1, NY - 1)]
    whole(rest, y_send.at[0], y_recv.at[0]).wait_recv()

    @pl.when(moved)
    def _():
        y_copy(band, 1).wait_recv()

    total = y_in[0].astype(F32)
    for s in range(1, NY):
        total = total + y_in[s].astype(F32)
    wout[...] = total
    store(2, wout, wgrad_hbm).start()

    east_copy(0, ml).wait_send()
    east_copy(1, ct).wait_send()
    west_copy().wait_send()
    for t in range(3):
        core_copy(t).wait_send()
        for d in range(1, NX):
            x_copy(t, d).wait_send()
    whole(z_in, z_send, z_recv).wait_send()
    whole(rest, y_send.at[0], y_recv.at[0]).wait_send()

    @pl.when(moved)
    def _():
        y_copy(band, 1).wait_send()

    store(0, gg, gg_hbm).wait()
    store(1, mg, mg_hbm).wait()
    store(2, wout, wgrad_hbm).wait()


def hand_over(a, b, c, a_out, b_out, c_out, a_held, b_held, c_held, in_sem, out_sem):
    quarter = GRID_ROWS // 4
    parts = [(a.at[pl.ds(i * quarter, quarter)], a_held.at[pl.ds(i * quarter, quarter)],
              a_out.at[pl.ds(i * quarter, quarter)]) for i in range(4)]
    parts += [(b, b_held, b_out), (c, c_held, c_out)]
    reads = [pltpu.make_async_copy(source, held, in_sem.at[i]) for i, (source, held, _) in enumerate(parts)]
    writes = [pltpu.make_async_copy(held, goal, out_sem.at[i]) for i, (_, held, goal) in enumerate(parts)]
    for copy in reads:
        copy.start()
    for read, write in zip(reads, writes):
        read.wait()
        write.start()
    for copy in writes:
        copy.wait()


def on_device(
    grid_latent, mesh_latent, mesh_cotangent, w_grid, w_mesh, w_out, edge_source, edge_target, edge_count
):
    edges = (SLOTS // LANES, LANES)
    dma = pltpu.SemaphoreType.DMA
    vmem = pltpu.VMEM
    anywhere = pl.BlockSpec(memory_space=pl.ANY)
    results = (
        jax.ShapeDtypeStruct((GRID_ROWS, D), BF16),
        jax.ShapeDtypeStruct((MESH_ROWS, D), BF16),
        jax.ShapeDtypeStruct((16, D), F32),
    )
    made = pl.pallas_call(
        kernel,
        out_shape=results,
        in_specs=[anywhere] * 8 + [pl.BlockSpec(memory_space=pltpu.SMEM)],
        out_specs=[anywhere] * 3,
        scratch_shapes=[
            vmem((GRID_ROWS, D), BF16),
            vmem((D, GRID_ROWS), BF16),
            vmem((D, D), BF16),
            vmem((D, D), BF16),
            vmem((D, D), BF16),
            vmem((TABLE, D), BF16),
            vmem((D, TABLE), BF16),
            vmem((TABLE, D), BF16),
            vmem(edges, jnp.int32),
            vmem(edges, jnp.int32),
            vmem((SLOTS, GRID_ROWS + TABLE), BF16),
            vmem((GRID_ROWS + TABLE, SLOTS), BF16),
            vmem((GRID_ROWS, D), BF16),
            vmem((TABLE, 2 * D), BF16),
            vmem((SLOTS, D), F32),
            vmem((SLOTS, 2 * D), BF16),
            vmem((GRID_ROWS, D), BF16),
            vmem((GRID_ROWS, D), BF16),
            vmem((MESH_ROWS, D), BF16),
            vmem((MESH_ROWS, D), F32),
            vmem((MESH_ROWS, D), BF16),
            vmem((MESH_ROWS, D), BF16),
            vmem((3, NC, NX, 64, D), BF16),
            vmem((3, NX, 64, D), BF16),
            vmem((3, NX, 64, D), BF16),
            vmem((3, NX - 1, 64, D), BF16),
            vmem((NZ, 16, D), BF16),
            vmem((NZ - 1, 16, D), BF16),
            vmem((16, D), BF16),
            vmem((NY, 16, D), BF16),
            vmem((16, D), F32),
            dma((8,)),
            dma((3,)),
            dma((2,)),
            dma((2,)),
            dma,
            dma,
            dma((3,)),
            dma((3,)),
            dma((3, NX - 1)),
            dma((3, NX - 1)),
            dma,
            dma,
            dma((2,)),
            dma((2,)),
        ],
        compiler_params=pltpu.CompilerParams(
            collective_id=0, has_side_effects=True, vmem_limit_bytes=56 * 1024 * 1024
        ),
        cost_estimate=pl.CostEstimate(flops=17_000_000_000, bytes_accessed=5_000_000, transcendentals=1_000_000),
    )(
        grid_latent, mesh_latent, mesh_cotangent, w_grid, w_mesh, w_out,
        edge_source.reshape(edges), edge_target.reshape(edges), edge_count,
    )
    return pl.pallas_call(
        hand_over,
        out_shape=results,
        in_specs=[anywhere] * 3,
        out_specs=[anywhere] * 3,
        scratch_shapes=[
            vmem((GRID_ROWS, D), BF16), vmem((MESH_ROWS, D), BF16), vmem((16, D), F32), dma((6,)), dma((6,)),
        ],
        cost_estimate=pl.CostEstimate(flops=0, bytes_accessed=2_400_000, transcendentals=0),
    )(*made)


def solution(mesh):
    in_specs = (
        P(("band", "lon"), None),
        P(("band", "lon"), None),
        P(("band", "lon"), None),
        P(),
        P(),
        P(),
        P(("band", "lon")),
        P(("band", "lon")),
        P(("band", "lon")),
    )
    out_specs = (P(("band", "lon"), None), P(("band", "lon"), None), P("lon", None))
    return jax.shard_map(
        on_device, mesh=mesh, in_specs=in_specs, out_specs=out_specs, check_vma=False
    )
```

time: 349 us -> 56.9 us (0.16)
  the two profiles are of different devices: /device:TPU:2 before, /device:TPU:1 now
where the time goes in v2:
time: 56.9 us; the launch traced here: 56.7 us
  Pallas kernels  55.4 us (97%)
  between operations  1.29 us (2%)
    pallas_call x1, Pallas kernels, on_device(): pl.pallas_call(kernel, out_shape=results, in_specs=[anywhere] * 8 + [pl.B...  53.3 us
    pallas_call x1, Pallas kernels, on_device(): pl.pallas_call(hand_over, out_shape=results, in_specs=[anywhere] * 3, out...  2.06 us

profile of v2, /device:TPU:1, one launch (start us, length us, event | category | flops | bytes accessed | tf_op | source)
XLA Modules:
  0.0 56.7 jit_solution(3531977226803480150)
XLA Ops:
  1.3 53.3 %shard_map.112 = (bf16[1024,512]{1,0:T(8,128)(2,1)}, bf16[128,512]{1,0:T(8,128)(2,1)}, f32[16,512]{1,0:T(8,128)}) custom-call(bf16[1024,512]{1,0:T(8,128)(2,1)} %gl_hbm.1, bf16[128,512]{1,0:T(8,128)(2,1)} %ml_hbm.1, bf16[128,512]{1,0:T(8,128)(2,1)} %ct_hbm.1, bf16[512,512]{1,0:T(8,128)(2,1)} %wg_hbm.1, bf16[512,512]{1,0:T(8,128)(2,1)} %wm_hbm.1, ...), custom_call_target="tpu_custom_call" | custom-call | flops 16999999488 | bytes 5000000 | tf_op jit(solution)/shard_map/pallas_call | solution.py:407
  54.6 2.1 %shard_map.113 = (bf16[1024,512]{1,0:T(8,128)(2,1)}, bf16[128,512]{1,0:T(8,128)(2,1)}, f32[16,512]{1,0:T(8,128)}) custom-call(bf16[1024,512]{1,0:T(8,128)(2,1)} %get-tuple-element.6.a, bf16[128,512]{1,0:T(8,128)(2,1)} %get-tuple-element.7.b, f32[16,512]{1,0:T(8,128)} %get-tuple-element.8.c), custom_call_target="tpu_custom_call" | custom-call | bytes 2400000 | tf_op jit(solution)/shard_map/pallas_call | solution.py:467

commit v3 on v2

--- a/solution.py
+++ b/solution.py
@@ -10,6 +10,7 @@
 F32 = jnp.float32
 
 D = 512
+HALF = 256
 GRID_ROWS = 1024
 MESH_ROWS = 128
 TABLE = 2 * MESH_ROWS
@@ -52,10 +53,11 @@
     gl, glt, wg, wm, wo, ml, mlt, ct, src, tgt,
     pick, pickt, table, mtable, pre, actgp, gpg, gg, mg,
     mine, tosend, west,
-    piece, core_in, mid, x_in, low, z_in, last, y_in, wout,
+    piece, core_in, mid, relay_in, x_in, grid_in, low, z_in, last, y_in, wout,
     load_sem, store_sem,
     east_send, east_recv, west_send, west_recv,
-    core_send, core_recv, x_send, x_recv, z_send, z_recv, y_send, y_recv,
+    core_send, core_recv, relay_send, relay_recv, x_send, x_recv, grid_send, grid_recv,
+    z_send, z_recv, y_send, y_recv,
 ):
     band = lax.axis_index("band")
     lon = lax.axis_index("lon")
@@ -138,40 +140,75 @@
         return pltpu.make_async_remote_copy(
             src_ref=piece.at[t, 1 - c],
             dst_ref=core_in.at[t],
-            send_sem=core_send.at[t],
-            recv_sem=core_recv.at[t],
+            send_sem=core_send.at[t, 0],
+            recv_sem=core_recv.at[t, 0],
             device_id=mate,
             device_id_type=MESH,
         )
 
-    def x_copy(t, d):
+    def core_half(h):
+        return pltpu.make_async_remote_copy(
+            src_ref=piece.at[GRID_TYPE, 1 - c, h],
+            dst_ref=core_in.at[GRID_TYPE, h],
+            send_sem=core_send.at[GRID_TYPE, h],
+            recv_sem=core_recv.at[GRID_TYPE, h],
+            device_id=mate,
+            device_id_type=MESH,
+        )
+
+    next_x = (x + 1) % NX
+    far_x = (x + 2) % NX
+    prev_x = (x + 3) % NX
+
+    def relay_copy(t, h):
+        return pltpu.make_async_remote_copy(
+            src_ref=mid.at[t, far_x, h],
+            dst_ref=relay_in.at[t - 1, h],
+            send_sem=relay_send.at[t - 1, h],
+            recv_sem=relay_recv.at[t - 1, h],
+            device_id=(band, lon_of(prev_x if h else next_x, z, c)),
+            device_id_type=MESH,
+        )
+
+    def x_copy(t, way):
+        there = prev_x if way else next_x
+        return pltpu.make_async_remote_copy(
+            src_ref=mid.at[t, there],
+            dst_ref=x_in.at[t - 1, way],
+            send_sem=x_send.at[t - 1, way],
+            recv_sem=x_recv.at[t - 1, way],
+            device_id=(band, lon_of(there, z, c)),
+            device_id_type=MESH,
+        )
+
+    def grid_copy(h, d):
         there = (x + d) % NX
         return pltpu.make_async_remote_copy(
-            src_ref=mid.at[t, there],
-            dst_ref=x_in.at[t, d - 1],
-            send_sem=x_send.at[t, d - 1],
-            recv_sem=x_recv.at[t, d - 1],
+            src_ref=mid.at[GRID_TYPE, there, h],
+            dst_ref=grid_in.at[h, d - 1],
+            send_sem=grid_send.at[h, d - 1],
+            recv_sem=grid_recv.at[h, d - 1],
             device_id=(band, lon_of(there, z, c)),
             device_id_type=MESH,
         )
 
-    def z_copy(there):
+    def z_copy(h, there):
         slot = (there + NZ - z + NZ - 1) % NZ
         return pltpu.make_async_remote_copy(
-            src_ref=low.at[there],
-            dst_ref=z_in.at[slot],
-            send_sem=z_send,
-            recv_sem=z_recv,
+            src_ref=low.at[h, there],
+            dst_ref=z_in.at[h, slot],
+            send_sem=z_send.at[h],
+            recv_sem=z_recv.at[h],
             device_id=(band, lon_of(x, there, c)),
             device_id_type=MESH,
         )
 
-    def y_copy(y, i):
-        return pltpu.make_async_remote_copy(
-            src_ref=last,
-            dst_ref=y_in.at[band],
-            send_sem=y_send.at[i],
-            recv_sem=y_recv.at[i],
+    def y_copy(h, y, i):
+        return pltpu.make_async_remote_copy(
+            src_ref=last.at[h],
+            dst_ref=y_in.at[h, band],
+            send_sem=y_send.at[h, i],
+            recv_sem=y_recv.at[h, i],
             device_id=(y, owner),
             device_id_type=MESH,
         )
@@ -252,44 +289,77 @@
 
     lax.fori_loop(0, SLOTS // 1024, edge, 0)
 
-    def put(t, values):
+    def put(t, h, values):
         values = values.astype(BF16)
         for cc in range(NC):
             for xx in range(NX):
                 for j in range(4):
                     first = block_row(t, cc, xx, j)
-                    piece[t, cc, xx, 16 * j:16 * (j + 1)] = values[first:first + 16]
-        core_copy(t).start()
-
-    def after_core(t):
-        core_copy(t).wait_recv()
+                    piece[t, cc, h, xx, 16 * j:16 * (j + 1)] = values[first:first + 16]
+
+    def after_core(t, h):
         for xx in range(NX):
-            total = piece[t, c, xx].astype(F32) + core_in[t, xx].astype(F32)
-            mid[t, xx] = total.astype(BF16)
-        for d in (2, 1, 3):
-            x_copy(t, d).start()
-
-    def after_x(t):
-        for d in range(1, NX):
-            x_copy(t, d).wait_recv()
-        total = mid[t, x].astype(F32)
-        for d in range(1, NX):
-            total = total + x_in[t, d - 1].astype(F32)
+            total = piece[t, c, h, xx].astype(F32) + core_in[t, h, xx].astype(F32)
+            mid[t, xx, h] = total.astype(BF16)
+
+    def to_z(t, h, total):
         total = total.astype(BF16)
         for j in range(4):
-            low[spot_z(x, t, j)] = total[16 * j:16 * (j + 1)]
+            low[h, spot_z(x, t, j)] = total[16 * j:16 * (j + 1)]
         for j in range(4):
             @pl.when(z != spot_z(x, t, j))
             def _():
-                z_copy(spot_z(x, t, j)).start()
+                z_copy(h, spot_z(x, t, j)).start()
+
+    def start_ring(t):
+        core_copy(t).wait_recv()
+        for h in range(2):
+            after_core(t, h)
+        for h in range(2):
+            relay_copy(t, h).start()
+
+    def step_ring(t):
+        for h in range(2):
+            relay_copy(t, h).wait_recv()
+            there = prev_x if h else next_x
+            total = mid[t, there, h].astype(F32) + relay_in[t - 1, h].astype(F32)
+            mid[t, there, h] = total.astype(BF16)
+        for way in range(2):
+            x_copy(t, way).start()
+
+    def end_ring(t):
+        for way in range(2):
+            x_copy(t, way).wait_recv()
+        for h in range(2):
+            total = mid[t, x, h].astype(F32) + x_in[t - 1, 0, h].astype(F32)
+            to_z(t, h, total + x_in[t - 1, 1, h].astype(F32))
+
+    def start_grid(h):
+        core_half(h).wait_recv()
+        after_core(GRID_TYPE, h)
+        for d in (2, 1, 3):
+            grid_copy(h, d).start()
+
+    def end_grid(h):
+        for d in range(1, NX):
+            grid_copy(h, d).wait_recv()
+        total = mid[GRID_TYPE, x, h].astype(F32)
+        for d in range(1, NX):
+            total = total + grid_in[h, d - 1].astype(F32)
+        to_z(GRID_TYPE, h, total)
 
     sums = dot(pickt[GRID_ROWS:, :], actgp[...])
     mine[...] = sums[:MESH_ROWS, D:]
     terms = sums[:, D:].astype(BF16)
     tosend[...] = terms[MESH_ROWS:]
     west_copy().start()
-    put(OUT_TYPE, dot(sums[:, :D].T.astype(BF16), ct[...]))
-    put(MESH_TYPE, dot(mlt[...], terms))
+    acts = sums[:, :D].T.astype(BF16)
+    for h in range(2):
+        put(OUT_TYPE, h, dot(acts, ct[:, h * HALF:(h + 1) * HALF]))
+    core_copy(OUT_TYPE).start()
+    for h in range(2):
+        put(MESH_TYPE, h, dot(mlt[...], terms[:, h * HALF:(h + 1) * HALF]))
+    core_copy(MESH_TYPE).start()
 
     def grid_side(first):
         def step(i, carry):
@@ -300,10 +370,12 @@
         lax.fori_loop(first, first + 1, step, 0)
 
     grid_side(0)
-    after_core(OUT_TYPE)
-    after_core(MESH_TYPE)
+    start_ring(OUT_TYPE)
+    start_ring(MESH_TYPE)
     grid_side(1)
-    put(GRID_TYPE, dot(glt[...], gpg[...]))
+    for h in range(2):
+        put(GRID_TYPE, h, dot(glt[...], gpg[:, h * HALF:(h + 1) * HALF]))
+        core_half(h).start()
 
     def grid_grads(first):
         def step(i, carry):
@@ -316,60 +388,70 @@
     def store(i, source, goal):
         return pltpu.make_async_copy(source, goal, store_sem.at[i])
 
+    step_ring(OUT_TYPE)
+    step_ring(MESH_TYPE)
+    start_grid(0)
+    start_grid(1)
     grid_grads(0)
-    after_core(GRID_TYPE)
-    after_x(OUT_TYPE)
-    after_x(MESH_TYPE)
+    end_ring(OUT_TYPE)
+    end_ring(MESH_TYPE)
     grid_grads(1)
     store(0, gg, gg_hbm).start()
     west_copy().wait_recv()
     mg[...] = dot_bt((mine[...] + west[...].astype(F32)).astype(BF16), wm[...]).astype(BF16)
     store(1, mg, mg_hbm).start()
-    after_x(GRID_TYPE)
-
-    whole(z_in, z_send, z_recv).wait_recv()
-    total = low[z].astype(F32)
-    for s in range(NZ - 1):
-        total = total + z_in[s].astype(F32)
-    last[...] = total.astype(BF16)
-
-    for d in (4, 3, 5, 2, 6, 1, 7):
-        y_copy((band + d) % NY, 0).start()
-
-    @pl.when(moved)
-    def _():
-        y_copy(band, 1).start()
-
-    @pl.when(jnp.logical_not(moved))
-    def _():
-        y_in[band] = last[...]
-
-    rest = y_in.at[pl.ds(1, NY - 1)]
-    whole(rest, y_send.at[0], y_recv.at[0]).wait_recv()
-
-    @pl.when(moved)
-    def _():
-        y_copy(band, 1).wait_recv()
-
-    total = y_in[0].astype(F32)
-    for s in range(1, NY):
-        total = total + y_in[s].astype(F32)
-    wout[...] = total
+    end_grid(0)
+    end_grid(1)
+
+    for h in range(2):
+        whole(z_in.at[h], z_send.at[h], z_recv.at[h]).wait_recv()
+        total = low[h, z].astype(F32)
+        for s in range(NZ - 1):
+            total = total + z_in[h, s].astype(F32)
+        last[h] = total.astype(BF16)
+        for d in (4, 3, 5, 2, 6, 1, 7):
+            y_copy(h, (band + d) % NY, 0).start()
+
+        @pl.when(moved)
+        def _():
+            y_copy(h, band, 1).start()
+
+        @pl.when(jnp.logical_not(moved))
+        def _():
+            y_in[h, band] = last[h]
+
+    for h in range(2):
+        rest = y_in.at[h, pl.ds(1, NY - 1)]
+        whole(rest, y_send.at[h, 0], y_recv.at[h, 0]).wait_recv()
+
+        @pl.when(moved)
+        def _():
+            y_copy(h, band, 1).wait_recv()
+
+        total = y_in[h, 0].astype(F32)
+        for s in range(1, NY):
+            total = total + y_in[h, s].astype(F32)
+        wout[:, h * HALF:(h + 1) * HALF] = total
     store(2, wout, wgrad_hbm).start()
 
     east_copy(0, ml).wait_send()
     east_copy(1, ct).wait_send()
     west_copy().wait_send()
-    for t in range(3):
+    for t in (MESH_TYPE, OUT_TYPE):
         core_copy(t).wait_send()
+        for h in range(2):
+            relay_copy(t, h).wait_send()
+            x_copy(t, h).wait_send()
+    for h in range(2):
+        core_half(h).wait_send()
         for d in range(1, NX):
-            x_copy(t, d).wait_send()
-    whole(z_in, z_send, z_recv).wait_send()
-    whole(rest, y_send.at[0], y_recv.at[0]).wait_send()
-
-    @pl.when(moved)
-    def _():
-        y_copy(band, 1).wait_send()
+            grid_copy(h, d).wait_send()
+        whole(z_in.at[h], z_send.at[h], z_recv.at[h]).wait_send()
+        whole(y_in.at[h, pl.ds(1, NY - 1)], y_send.at[h, 0], y_recv.at[h, 0]).wait_send()
+
+        @pl.when(moved)
+        def _():
+            y_copy(h, band, 1).wait_send()
 
     store(0, gg, gg_hbm).wait()
     store(1, mg, mg_hbm).wait()
@@ -432,14 +514,16 @@
             vmem((MESH_ROWS, D), F32),
             vmem((MESH_ROWS, D), BF16),
             vmem((MESH_ROWS, D), BF16),
-            vmem((3, NC, NX, 64, D), BF16),
-            vmem((3, NX, 64, D), BF16),
-            vmem((3, NX, 64, D), BF16),
-            vmem((3, NX - 1, 64, D), BF16),
-            vmem((NZ, 16, D), BF16),
-            vmem((NZ - 1, 16, D), BF16),
-            vmem((16, D), BF16),
-            vmem((NY, 16, D), BF16),
+            vmem((3, NC, 2, NX, 64, HALF), BF16),
+            vmem((3, 2, NX, 64, HALF), BF16),
+            vmem((3, NX, 2, 64, HALF), BF16),
+            vmem((2, 2, 64, HALF), BF16),
+            vmem((2, 2, 2, 64, HALF), BF16),
+            vmem((2, NX - 1, 64, HALF), BF16),
+            vmem((2, NZ, 16, HALF), BF16),
+            vmem((2, NZ - 1, 16, HALF), BF16),
+            vmem((2, 16, HALF), BF16),
+            vmem((2, NY, 16, HALF), BF16),
             vmem((16, D), F32),
             dma((8,)),
             dma((3,)),
@@ -447,14 +531,18 @@
             dma((2,)),
             dma,
             dma,
-            dma((3,)),
-            dma((3,)),
-            dma((3, NX - 1)),
-            dma((3, NX - 1)),
-            dma,
-            dma,
+            dma((3, 2)),
+            dma((3, 2)),
+            dma((2, 2)),
+            dma((2, 2)),
+            dma((2, 2)),
+            dma((2, 2)),
+            dma((2, NX - 1)),
+            dma((2, NX - 1)),
             dma((2,)),
             dma((2,)),
+            dma((2, 2)),
+            dma((2, 2)),
         ],
         compiler_params=pltpu.CompilerParams(
             collective_id=0, has_side_effects=True, vmem_limit_bytes=56 * 1024 * 1024

time: 56.9 us -> 56.5 us (level)
  the two profiles are of different devices: /device:TPU:1 before, /device:TPU:2 now
where the time goes in v3:
time: 56.5 us; the launch traced here: 56.3 us
  Pallas kernels  55 us (97%)
  between operations  1.29 us (2%)
    pallas_call x1, Pallas kernels, on_device(): pl.pallas_call(kernel, out_shape=results, in_specs=[anywhere] * 8 + [pl.B...  53 us
    pallas_call x1, Pallas kernels, on_device(): pl.pallas_call(hand_over, out_shape=results, in_specs=[anywhere] * 3, out...  2.06 us

profile of v3, /device:TPU:2, one launch (start us, length us, event | category | flops | bytes accessed | tf_op | source)
XLA Modules:
  0.0 56.3 jit_solution(15191655204541711534)
XLA Ops:
  1.3 53.0 %shard_map.112 = (bf16[1024,512]{1,0:T(8,128)(2,1)}, bf16[128,512]{1,0:T(8,128)(2,1)}, f32[16,512]{1,0:T(8,128)}) custom-call(bf16[1024,512]{1,0:T(8,128)(2,1)} %gl_hbm.1, bf16[128,512]{1,0:T(8,128)(2,1)} %ml_hbm.1, bf16[128,512]{1,0:T(8,128)(2,1)} %ct_hbm.1, bf16[512,512]{1,0:T(8,128)(2,1)} %wg_hbm.1, bf16[512,512]{1,0:T(8,128)(2,1)} %wm_hbm.1, ...), custom_call_target="tpu_custom_call" | custom-call | flops 16999999488 | bytes 5000000 | tf_op jit(solution)/shard_map/pallas_call | solution.py:489
  54.2 2.1 %shard_map.113 = (bf16[1024,512]{1,0:T(8,128)(2,1)}, bf16[128,512]{1,0:T(8,128)(2,1)}, f32[16,512]{1,0:T(8,128)}) custom-call(bf16[1024,512]{1,0:T(8,128)(2,1)} %get-tuple-element.6.a, bf16[128,512]{1,0:T(8,128)(2,1)} %get-tuple-element.7.b, f32[16,512]{1,0:T(8,128)} %get-tuple-element.8.c), custom_call_target="tpu_custom_call" | custom-call | bytes 2400000 | tf_op jit(solution)/shard_map/pallas_call | solution.py:555

commit v4 on v3

--- a/solution.py
+++ b/solution.py
@@ -18,6 +18,7 @@
 LANES = 128
 NX, NY, NZ, NC = 4, 8, 12, 2
 N_LON = NX * NZ * NC
+ROUNDS = NZ // 2 - 1
 GRID_TYPE, MESH_TYPE, OUT_TYPE = 0, 1, 2
 SPOTS = (
     ((0, 0), (0, 1), (0, 2), (1, 0)),
@@ -54,7 +55,7 @@
     pick, pickt, table, mtable, pre, actgp, gpg, gg, mg,
     mine, tosend, west,
     piece, core_in, mid, relay_in, x_in, grid_in, low, z_in, last, y_in, wout,
-    load_sem, store_sem,
+    load_sem, store_sem, token,
     east_send, east_recv, west_send, west_recv,
     core_send, core_recv, relay_send, relay_recv, x_send, x_recv, grid_send, grid_recv,
     z_send, z_recv, y_send, y_recv,
@@ -66,7 +67,6 @@
     c = lon % NC
     moved = z % NX != 0
     owner = lon_of((x + NZ - z) % NX, z, c)
-    summer = lon_of((x + z) % NX, z, c)
     to_west = (band, (lon + N_LON - 1) % N_LON)
     to_east = (band, (lon + 1) % N_LON)
     mate = (band, lon_of(x, z, 1 - c))
@@ -75,12 +75,12 @@
         return pltpu.make_async_copy(source, target, load_sem.at[i])
 
     loads = [
-        load(0, src_hbm, src),
-        load(1, tgt_hbm, tgt),
-        load(2, gl_hbm, gl),
-        load(3, wg_hbm, wg),
-        load(4, ml_hbm, ml.at[pl.ds(0, MESH_ROWS)]),
-        load(5, ct_hbm, ct.at[pl.ds(0, MESH_ROWS)]),
+        load(0, ml_hbm, ml.at[pl.ds(0, MESH_ROWS)]),
+        load(1, ct_hbm, ct.at[pl.ds(0, MESH_ROWS)]),
+        load(2, src_hbm, src),
+        load(3, tgt_hbm, tgt),
+        load(4, gl_hbm, gl),
+        load(5, wg_hbm, wg),
         load(6, wm_hbm, wm),
         load(7, wo_hbm, wo),
     ]
@@ -98,23 +98,21 @@
     for d in range(1, NX):
         greet((band, lon_of((x + d) % NX, z, c)))
 
-    def greet_z(d, carry):
-        greet((band, lon_of(x, (z + d) % NZ, c)))
-        return carry
-
-    lax.fori_loop(1, NZ, greet_z, 0)
-
-    def greet_y(d, carry):
-        greet(((band + d) % NY, owner))
-        greet(((band + d) % NY, summer))
-        return carry
-
-    lax.fori_loop(1, NY, greet_y, 0)
-
-    @pl.when(moved)
-    def _():
-        greet((band, owner))
-        greet((band, summer))
+    beside = [
+        (band, lon_of(x, (z + 1) % NZ, c)),
+        (band, lon_of(x, (z + NZ - 1) % NZ, c)),
+        ((band + 1) % NY, lon),
+        ((band + NY - 1) % NY, lon),
+    ]
+    for device in beside:
+        greet(device)
+
+    def tell(i):
+        for device in beside:
+            pl.semaphore_signal(token.at[i], inc=1, device_id=device, device_id_type=MESH)
+
+    def hear(i):
+        pl.semaphore_wait(token.at[i], len(beside))
 
     def east_copy(i, ref):
         return pltpu.make_async_remote_copy(
@@ -170,13 +168,13 @@
             device_id_type=MESH,
         )
 
-    def x_copy(t, way):
+    def x_copy(t, way, h):
         there = prev_x if way else next_x
         return pltpu.make_async_remote_copy(
-            src_ref=mid.at[t, there],
-            dst_ref=x_in.at[t - 1, way],
-            send_sem=x_send.at[t - 1, way],
-            recv_sem=x_recv.at[t - 1, way],
+            src_ref=mid.at[t, there, h],
+            dst_ref=x_in.at[t - 1, way, h],
+            send_sem=x_send.at[t - 1, way, h],
+            recv_sem=x_recv.at[t - 1, way, h],
             device_id=(band, lon_of(there, z, c)),
             device_id_type=MESH,
         )
@@ -221,6 +219,13 @@
 
     loads[0].wait()
     loads[1].wait()
+    pl.semaphore_wait(barrier, 3 + (NX - 1) + len(beside))
+    east_copy(0, ml).start()
+    east_copy(1, ct).start()
+    tell(0)
+
+    loads[2].wait()
+    loads[3].wait()
     slot = lax.broadcasted_iota(jnp.int32, (SLOTS // LANES, LANES), 0) * LANES
     slot = slot + lax.broadcasted_iota(jnp.int32, (SLOTS // LANES, LANES), 1)
     target = tgt[...]
@@ -246,16 +251,14 @@
 
     lax.fori_loop(0, SLOTS // LANES, build, 0)
 
-    loads[2].wait()
-    loads[3].wait()
-
+    hear(0)
+    tell(1)
+
+    loads[4].wait()
+    loads[5].wait()
     table[...] = dot(gl[...], wg[...]).astype(BF16)
-
-    for i in range(4, 8):
-        loads[i].wait()
-    pl.semaphore_wait(barrier, 3 + (NX - 1) + (NZ - 1) + 2 * (NY - 1) + jnp.where(moved, 2, 0))
-    east_copy(0, ml).start()
-    east_copy(1, ct).start()
+    hear(1)
+    tell(2)
 
     def gather(i, carry):
         rows = pl.ds(pl.multiple_of(i * 1024, 1024), 1024)
@@ -263,6 +266,8 @@
         return carry
 
     lax.fori_loop(0, SLOTS // 1024, gather, 0)
+    hear(2)
+    tell(3)
 
     def turn(i, carry):
         rows = pl.ds(pl.multiple_of(i * 256, 256), 256)
@@ -271,6 +276,8 @@
 
     lax.fori_loop(0, GRID_ROWS // 256, turn, 0)
 
+    loads[6].wait()
+    loads[7].wait()
     east_copy(0, ml).wait_recv()
     east_copy(1, ct).wait_recv()
     mlt[...] = ml[...].T
@@ -288,6 +295,8 @@
         return carry
 
     lax.fori_loop(0, SLOTS // 1024, edge, 0)
+    hear(3)
+    tell(4)
 
     def put(t, h, values):
         values = values.astype(BF16)
@@ -317,6 +326,8 @@
             after_core(t, h)
         for h in range(2):
             relay_copy(t, h).start()
+        for h in range(2):
+            x_copy(t, 1 - h, h).start()
 
     def step_ring(t):
         for h in range(2):
@@ -324,13 +335,12 @@
             there = prev_x if h else next_x
             total = mid[t, there, h].astype(F32) + relay_in[t - 1, h].astype(F32)
             mid[t, there, h] = total.astype(BF16)
-        for way in range(2):
-            x_copy(t, way).start()
+            x_copy(t, h, h).start()
 
     def end_ring(t):
-        for way in range(2):
-            x_copy(t, way).wait_recv()
         for h in range(2):
+            x_copy(t, 0, h).wait_recv()
+            x_copy(t, 1, h).wait_recv()
             total = mid[t, x, h].astype(F32) + x_in[t - 1, 0, h].astype(F32)
             to_z(t, h, total + x_in[t - 1, 1, h].astype(F32))
 
@@ -393,6 +403,7 @@
     start_grid(0)
     start_grid(1)
     grid_grads(0)
+    hear(4)
     end_ring(OUT_TYPE)
     end_ring(MESH_TYPE)
     grid_grads(1)
@@ -441,7 +452,8 @@
         core_copy(t).wait_send()
         for h in range(2):
             relay_copy(t, h).wait_send()
-            x_copy(t, h).wait_send()
+            x_copy(t, 0, h).wait_send()
+            x_copy(t, 1, h).wait_send()
     for h in range(2):
         core_half(h).wait_send()
         for d in range(1, NX):
@@ -527,6 +539,7 @@
             vmem((16, D), F32),
             dma((8,)),
             dma((3,)),
+            pltpu.SemaphoreType.REGULAR((ROUNDS,)),
             dma((2,)),
             dma((2,)),
             dma,
@@ -535,8 +548,8 @@
             dma((3, 2)),
             dma((2, 2)),
             dma((2, 2)),
-            dma((2, 2)),
-            dma((2, 2)),
+            dma((2, 2, 2)),
+            dma((2, 2, 2)),
             dma((2, NX - 1)),
             dma((2, NX - 1)),
             dma((2,)),

time: 56.5 us -> 54.5 us (0.965)
  Pallas kernels: 55 us -> 53 us
    pallas_call x1, Pallas kernels: 53 us -> 50.9 us  [on_device(): pl.pallas_call(kernel, out_shape=results, in_specs=[anywhere] * 8 + [pl.B...]
where the time goes in v4:
time: 54.5 us; the launch traced here: 54.3 us
  Pallas kernels  53 us (97%)
  between operations  1.29 us (2%)
    pallas_call x1, Pallas kernels, on_device(): pl.pallas_call(kernel, out_shape=results, in_specs=[anywhere] * 8 + [pl.B...  50.9 us
    pallas_call x1, Pallas kernels, on_device(): pl.pallas_call(hand_over, out_shape=results, in_specs=[anywhere] * 3, out...  2.06 us

profile of v4, /device:TPU:2, one launch (start us, length us, event | category | flops | bytes accessed | tf_op | source)
XLA Modules:
  0.0 54.3 jit_solution(8315358582443208006)
XLA Ops:
  1.3 50.9 %shard_map.112 = (bf16[1024,512]{1,0:T(8,128)(2,1)}, bf16[128,512]{1,0:T(8,128)(2,1)}, f32[16,512]{1,0:T(8,128)}) custom-call(bf16[1024,512]{1,0:T(8,128)(2,1)} %gl_hbm.1, bf16[128,512]{1,0:T(8,128)(2,1)} %ml_hbm.1, bf16[128,512]{1,0:T(8,128)(2,1)} %ct_hbm.1, bf16[512,512]{1,0:T(8,128)(2,1)} %wg_hbm.1, bf16[512,512]{1,0:T(8,128)(2,1)} %wm_hbm.1, ...), custom_call_target="tpu_custom_call" | custom-call | flops 16999999488 | bytes 5000000 | tf_op jit(solution)/shard_map/pallas_call | solution.py:501
  52.2 2.1 %shard_map.113 = (bf16[1024,512]{1,0:T(8,128)(2,1)}, bf16[128,512]{1,0:T(8,128)(2,1)}, f32[16,512]{1,0:T(8,128)}) custom-call(bf16[1024,512]{1,0:T(8,128)(2,1)} %get-tuple-element.6.a, bf16[128,512]{1,0:T(8,128)(2,1)} %get-tuple-element.7.b, f32[16,512]{1,0:T(8,128)} %get-tuple-element.8.c), custom_call_target="tpu_custom_call" | custom-call | bytes 2400000 | tf_op jit(solution)/shard_map/pallas_call | solution.py:568

commit v5 on v4

--- a/solution.py
+++ b/solution.py
@@ -16,6 +16,7 @@
 TABLE = 2 * MESH_ROWS
 SLOTS = 2048
 LANES = 128
+CHUNK = 512
 NX, NY, NZ, NC = 4, 8, 12, 2
 N_LON = NX * NZ * NC
 ROUNDS = NZ // 2 - 1
@@ -234,12 +235,13 @@
     row = jnp.where(here, target - start, MESH_ROWS + (target & (MESH_ROWS - 1)))
     tgt[...] = jnp.where(slot < cnt[0], row + GRID_ROWS, -1)
 
-    def build(r, carry):
-        columns = pl.ds(pl.multiple_of(r * LANES, LANES), LANES)
-        down = lax.broadcasted_iota(jnp.int32, (LANES, LANES), 0).astype(jnp.int16)
-        across = lax.broadcasted_iota(jnp.int32, (LANES, LANES), 1).astype(jnp.int16)
-        sb = jnp.broadcast_to(src[pl.ds(r, 1), :], (LANES, LANES)).astype(jnp.int16)
-        tb = jnp.broadcast_to(tgt[pl.ds(r, 1), :], (LANES, LANES)).astype(jnp.int16)
+    across = lax.broadcasted_iota(jnp.int32, (LANES, LANES), 1).astype(jnp.int16)
+    down = lax.broadcasted_iota(jnp.int32, (LANES, LANES), 0).astype(jnp.int16)
+
+    def build(r):
+        columns = slice(r * LANES, (r + 1) * LANES)
+        sb = jnp.broadcast_to(src[r:r + 1, :], (LANES, LANES)).astype(jnp.int16)
+        tb = jnp.broadcast_to(tgt[r:r + 1, :], (LANES, LANES)).astype(jnp.int16)
         st = sb.T
         tt = tb.T
         for k in range((GRID_ROWS + TABLE) // LANES):
@@ -247,9 +249,12 @@
             pickt[k * LANES:(k + 1) * LANES, columns] = jnp.where(one, jnp.ones((), BF16), jnp.zeros((), BF16))
             one = (st if k < GRID_ROWS // LANES else tt) == across + jnp.int16(k * LANES)
             pick[columns, k * LANES:(k + 1) * LANES] = jnp.where(one, jnp.ones((), BF16), jnp.zeros((), BF16))
-        return carry
-
-    lax.fori_loop(0, SLOTS // LANES, build, 0)
+
+    def build_chunk(i):
+        for r in range(CHUNK // LANES):
+            build(i * (CHUNK // LANES) + r)
+
+    build_chunk(0)
 
     hear(0)
     tell(1)
@@ -257,24 +262,20 @@
     loads[4].wait()
     loads[5].wait()
     table[...] = dot(gl[...], wg[...]).astype(BF16)
+    build_chunk(1)
     hear(1)
     tell(2)
 
-    def gather(i, carry):
-        rows = pl.ds(pl.multiple_of(i * 1024, 1024), 1024)
-        pre[rows, :] = dot(pick[rows, :GRID_ROWS], table[...])
-        return carry
-
-    lax.fori_loop(0, SLOTS // 1024, gather, 0)
+    for first in range(0, SLOTS, CHUNK):
+        pre[first:first + CHUNK, :] = dot(pick[first:first + CHUNK, :GRID_ROWS], table[...])
+        if first + 2 * CHUNK < SLOTS:
+            build_chunk(first // CHUNK + 2)
+        else:
+            turned = slice(GRID_ROWS * (first - SLOTS + 2 * CHUNK) // (2 * CHUNK), GRID_ROWS * (first - SLOTS + 3 * CHUNK) // (2 * CHUNK))
+            glt[:, turned] = gl[turned, :].T
     hear(2)
     tell(3)
 
-    def turn(i, carry):
-        rows = pl.ds(pl.multiple_of(i * 256, 256), 256)
-        glt[:, rows] = gl[rows, :].T
-        return carry
-
-    lax.fori_loop(0, GRID_ROWS // 256, turn, 0)
 
     loads[6].wait()
     loads[7].wait()
@@ -284,17 +285,15 @@
     mtable[:, :D] = dot(ml[...], wm[...]).astype(BF16)
     mtable[:, D:] = dot_bt(ct[...], wo[...]).astype(BF16)
 
-    def edge(i, carry):
-        rows = pl.ds(pl.multiple_of(i * 1024, 1024), 1024)
+    for first in range(0, SLOTS, 512):
+        rows = slice(first, first + 512)
         both = dot(pick[rows, GRID_ROWS:], mtable[...])
         value = pre[rows, :] + both[:, :D]
         sig = 0.5 * jnp.tanh(0.5 * value) + 0.5
         act = value * sig
         actgp[rows, :D] = act.astype(BF16)
         actgp[rows, D:] = (both[:, D:] * (sig + act * (1.0 - sig))).astype(BF16)
-        return carry
-
-    lax.fori_loop(0, SLOTS // 1024, edge, 0)
+
     hear(3)
     tell(4)
 

time: 54.5 us -> 53.7 us (0.985)
  the two profiles are of different devices: /device:TPU:2 before, /device:TPU:128 now
where the time goes in v5:
time: 53.7 us; the launch traced here: 53.5 us
  Pallas kernels  52.2 us (97%)
  between operations  1.29 us (2%)
    pallas_call x1, Pallas kernels, on_device(): pl.pallas_call(kernel, out_shape=results, in_specs=[anywhere] * 8 + [pl.B...  50.1 us
    pallas_call x1, Pallas kernels, on_device(): pl.pallas_call(hand_over, out_shape=results, in_specs=[anywhere] * 3, out...  2.06 us

profile of v5, /device:TPU:128, one launch (start us, length us, event | category | flops | bytes accessed | tf_op | source)
XLA Modules:
  0.0 53.5 jit_solution(6390350677266069919)
XLA Ops:
  1.3 50.1 %shard_map.112 = (bf16[1024,512]{1,0:T(8,128)(2,1)}, bf16[128,512]{1,0:T(8,128)(2,1)}, f32[16,512]{1,0:T(8,128)}) custom-call(bf16[1024,512]{1,0:T(8,128)(2,1)} %gl_hbm.1, bf16[128,512]{1,0:T(8,128)(2,1)} %ml_hbm.1, bf16[128,512]{1,0:T(8,128)(2,1)} %ct_hbm.1, bf16[512,512]{1,0:T(8,128)(2,1)} %wg_hbm.1, bf16[512,512]{1,0:T(8,128)(2,1)} %wm_hbm.1, ...), custom_call_target="tpu_custom_call" | custom-call | flops 16999999488 | bytes 5000000 | tf_op jit(solution)/shard_map/pallas_call | solution.py:500
  51.4 2.1 %shard_map.113 = (bf16[1024,512]{1,0:T(8,128)(2,1)}, bf16[128,512]{1,0:T(8,128)(2,1)}, f32[16,512]{1,0:T(8,128)}) custom-call(bf16[1024,512]{1,0:T(8,128)(2,1)} %get-tuple-element.6.a, bf16[128,512]{1,0:T(8,128)(2,1)} %get-tuple-element.7.b, f32[16,512]{1,0:T(8,128)} %get-tuple-element.8.c), custom_call_target="tpu_custom_call" | custom-call | bytes 2400000 | tf_op jit(solution)/shard_map/pallas_call | solution.py:567

commit v6 on v5

--- a/solution.py
+++ b/solution.py
@@ -370,13 +370,9 @@
         put(MESH_TYPE, h, dot(mlt[...], terms[:, h * HALF:(h + 1) * HALF]))
     core_copy(MESH_TYPE).start()
 
-    def grid_side(first):
-        def step(i, carry):
-            rows = pl.ds(pl.multiple_of(i * 512, 512), 512)
-            gpg[rows, :] = dot(pickt[rows, :], actgp[:, D:]).astype(BF16)
-            return carry
-
-        lax.fori_loop(first, first + 1, step, 0)
+    def grid_side(i):
+        rows = slice(i * CHUNK, (i + 1) * CHUNK)
+        gpg[rows, :] = dot(pickt[rows, :], actgp[:, D:]).astype(BF16)
 
     grid_side(0)
     start_ring(OUT_TYPE)
@@ -405,13 +401,13 @@
     hear(4)
     end_ring(OUT_TYPE)
     end_ring(MESH_TYPE)
+    end_grid(0)
+    end_grid(1)
     grid_grads(1)
     store(0, gg, gg_hbm).start()
     west_copy().wait_recv()
     mg[...] = dot_bt((mine[...] + west[...].astype(F32)).astype(BF16), wm[...]).astype(BF16)
     store(1, mg, mg_hbm).start()
-    end_grid(0)
-    end_grid(1)
 
     for h in range(2):
         whole(z_in.at[h], z_send.at[h], z_recv.at[h]).wait_recv()

time: 53.7 us -> 53.5 us (level)
  the two profiles are of different devices: /device:TPU:128 before, /device:TPU:8 now
where the time goes in v6:
time: 53.5 us; the launch traced here: 53.3 us
  Pallas kernels  52.1 us (97%)
  between operations  1.29 us (2%)
    pallas_call x1, Pallas kernels, on_device(): pl.pallas_call(kernel, out_shape=results, in_specs=[anywhere] * 8 + [pl.B...  50 us
    pallas_call x1, Pallas kernels, on_device(): pl.pallas_call(hand_over, out_shape=results, in_specs=[anywhere] * 3, out...  2.06 us

profile of v6, /device:TPU:8, one launch (start us, length us, event | category | flops | bytes accessed | tf_op | source)
XLA Modules:
  0.0 53.3 jit_solution(17162306541120839255)
XLA Ops:
  1.3 50.0 %shard_map.112 = (bf16[1024,512]{1,0:T(8,128)(2,1)}, bf16[128,512]{1,0:T(8,128)(2,1)}, f32[16,512]{1,0:T(8,128)}) custom-call(bf16[1024,512]{1,0:T(8,128)(2,1)} %gl_hbm.1, bf16[128,512]{1,0:T(8,128)(2,1)} %ml_hbm.1, bf16[128,512]{1,0:T(8,128)(2,1)} %ct_hbm.1, bf16[512,512]{1,0:T(8,128)(2,1)} %wg_hbm.1, bf16[512,512]{1,0:T(8,128)(2,1)} %wm_hbm.1, ...), custom_call_target="tpu_custom_call" | custom-call | flops 16999999488 | bytes 5000000 | tf_op jit(solution)/shard_map/pallas_call | solution.py:496
  51.3 2.1 %shard_map.113 = (bf16[1024,512]{1,0:T(8,128)(2,1)}, bf16[128,512]{1,0:T(8,128)(2,1)}, f32[16,512]{1,0:T(8,128)}) custom-call(bf16[1024,512]{1,0:T(8,128)(2,1)} %get-tuple-element.6.a, bf16[128,512]{1,0:T(8,128)(2,1)} %get-tuple-element.7.b, f32[16,512]{1,0:T(8,128)} %get-tuple-element.8.c), custom_call_target="tpu_custom_call" | custom-call | bytes 2400000 | tf_op jit(solution)/shard_map/pallas_call | solution.py:563
